TPU v7x, 32 devices: a whole 2x2x4 slice. The times are simulated.
32 devices in a mesh: tm: 4 (over y, x), space: 8 (over z, core).
Axes of the slice: x: 2, y: 2, z: 4, core: 2. Of those that a mesh axis runs over, the one named last changes fastest.
Arguments:
- guess: float32 [8, 3, 96, 64, 128], P('tm', None, 'space'), may hold values from -6 to 6
- source: float32 [8, 3, 96, 64, 128], P('tm', None, 'space'), may hold values from -6 to 6
- regions: int32 [96, 64, 128], P('space'), may hold values from 0 to 3
- conductance: float32 [4], replicated, may hold values from 8 to 32
- reluct: float32 [4], replicated, may hold values from 0.25 to 2
Outputs:
- field: float32 [8, 3, 96, 64, 128], P('tm', None, 'space')
- coarse_residual: float32 [4, 3, 96, 64, 128], P('tm', None, 'space')
Inputs may be any that keep to these rules, and one draw needn't show every extreme that they name: `regions`: a region id per cell.
All inputs are finite; a program needn't handle non-finite values.
Results may differ from a plain program's by a relative error of at most 0.0001.
Values sent between devices are 32-bit elements; how exact they have to be, the bound alone decides.
A program may use at most 128 MiB of HBM per device.

v0:
```python
import jax
import jax.numpy as jnp
from jax import lax
from jax.sharding import PartitionSpec as P

PICARD = 2


def extended_2(x, sides, width):
    for axis, dim in sides:
        count, length = (lax.axis_size(axis), x.shape[dim])
        up = [(i, (i + 1) % count) for i in range(count - 1)]
        down = [(j, i) for i, j in up]
        last = lax.slice_in_dim(x, length - width, length, axis=dim)
        leading = lax.slice_in_dim(x, 0, width, axis=dim)
        before = lax.ppermute(last, axis, up)
        after = lax.ppermute(leading, axis, down)
        x = jnp.concatenate([before, x, after], axis=dim)
    return x


def shifted(block, axis, distance):
    devices = range(lax.axis_size(axis))
    route = [((i - distance) % len(devices), i) for i in devices]
    return lax.ppermute(block, axis, route)


def material(regions, table):
    ids = jnp.arange(table.shape[0]).reshape(-1, 1, 1, 1)
    return jnp.sum(
        jnp.where(regions[None] == ids, table.reshape(-1, 1, 1, 1), jnp.float32(0.0)), axis=0
    )


def neighbour_sum(extended):
    first = extended[:, 2:] + extended[:, :-2]
    centre = extended[:, 1:-1]
    padded = jnp.pad(centre, ((0, 0), (0, 0), (1, 1), (1, 1)))
    second = padded[:, :, 2:, 1:-1] + padded[:, :, :-2, 1:-1]
    third = padded[:, :, 1:-1, 2:] + padded[:, :, 1:-1, :-2]
    return first + second + third


def rim_one(state):
    return extended_2(state, (("space", 1),), 1)


def fine_update(extended, old, force, cond, base_nu):
    centre = extended[:, 1:-1]
    square = jnp.sum(centre * centre, axis=0)
    nu = (base_nu * (1.0 + 0.5 * square / (1.0 + square)))[None]
    return (cond * old + force + nu * neighbour_sum(extended)) / (cond + 6.0 * nu)


def body(guess, source, regions, conductance, reluct):
    steps = guess.shape[0]
    cond = material(regions, conductance)
    base_nu = material(regions, reluct)

    def advance(old, force):
        state = old
        for sweep in range(PICARD):
            state = fine_update(rim_one(state), old, force, cond, base_nu)
        return state

    cond_coarse = cond / steps

    def previous_end(last):
        return shifted(last, "tm", 1)

    points = [guess[i] for i in range(steps)]
    forces = [source[i] for i in range(steps)]

    def relax_f(points):
        points = list(points)
        points[1] = advance(points[0], forces[1])
        return points

    points = relax_f(points)
    points[0] = advance(previous_end(points[steps - 1]), forces[0])
    points = relax_f(points)
    residual = advance(previous_end(points[steps - 1]), forces[0]) - points[0]
    slices = lax.axis_size("tm")
    correction = jnp.zeros_like(residual)
    for k in range(slices):
        flat = shifted(correction, "tm", 1)
        coarse_state = flat
        for coarse_sweep in range(PICARD):
            coarse_state = (cond_coarse * flat + base_nu * neighbour_sum(rim_one(coarse_state))) / (
                cond_coarse + 6.0 * base_nu
            )
        correction = coarse_state + residual
    points[0] = points[0] + correction
    points = relax_f(points)
    return (jnp.stack(points, axis=0), residual[None])


def solution(mesh):
    in_specs = (
        P("tm", None, "space", None, None),
        P("tm", None, "space", None, None),
        P("space", None, None),
        P(),
        P(),
    )
    out_specs = (P("tm", None, "space", None, None), P("tm", None, "space", None, None))
    return jax.shard_map(body, mesh=mesh, in_specs=in_specs, out_specs=out_specs, check_vma=False)
```

profile of v0, /device:TPU:7, one launch (start us, length us, event | category | flops | bytes accessed | tf_op | source)
XLA Modules:
  0.0 289.0 jit_solution(2255926557935272913)
XLA Ops:
  0.6 1.5 slice_bitcast_fusion
  2.2 2.7 collective-permute-start
  5.0 3.1 %collective-permute-start.1 = (f32[3,1,64,128]{3,2,1,0:T(8,128)S(1)}, f32[3,1,64,128]{3,2,1,0:T(8,128)S(1)}, u32[]{:S(2)}, u32[]{:S(2)}) collective-permute-start(f32[3,1,64,128]{3,2,1,0:T(8,128)S(1)} %get-tuple-element.75), channel_id=1, source_target_pairs={{0,1},{1,2},{2,3},{3,4},{4,5},{5,6},{6,7},{8,9},{9,10},{10,11},{11... | collective-permute-start | bytes 294920 | tf_op jit(solution)/shard_map/ppermute | solution.py:16
  10.8 1.9 collective-permute-start.2
  12.7 4.1 %collective-permute-start.3 = (f32[3,1,64,128]{3,2,1,0:T(8,128)S(1)}, f32[3,1,64,128]{3,2,1,0:T(8,128)S(1)}, u32[]{:S(2)}, u32[]{:S(2)}) collective-permute-start(f32[3,1,64,128]{3,2,1,0:T(8,128)S(1)} %get-tuple-element.73), channel_id=1, source_target_pairs={{0,1},{1,2},{2,3},{3,4},{4,5},{5,6},{6,7},{8,9},{9,10},{10,11},{11... | collective-permute-start | bytes 294920 | tf_op jit(solution)/shard_map/ppermute | solution.py:16
  17.2 1.3 collective-permute-done.3
  19.7 1.3 collective-permute-start.9
  21.0 26.5 %collective-permute-done.4 = f32[3,12,64,128]{3,2,1,0:T(8,128)S(1)} collective-permute-done((f32[3,12,64,128]{3,2,1,0:T(8,128)S(1)}, f32[3,12,64,128]{3,2,1,0:T(8,128)S(1)}, u32[]{:S(2)}, u32[]{:S(2)}) %collective-permute-start.4) | collective-permute-done | bytes 1179680 | tf_op jit(solution)/shard_map/ppermute | solution.py:25
  47.5 1.9 collective-permute-start.5
  49.4 5.2 %collective-permute-start.6 = (f32[3,1,64,128]{3,2,1,0:T(8,128)S(1)}, f32[3,1,64,128]{3,2,1,0:T(8,128)S(1)}, u32[]{:S(2)}, u32[]{:S(2)}) collective-permute-start(f32[3,1,64,128]{3,2,1,0:T(8,128)S(1)} %get-tuple-element.71), channel_id=1, source_target_pairs={{0,1},{1,2},{2,3},{3,4},{4,5},{5,6},{6,7},{8,9},{9,10},{10,11},{11... | collective-permute-start | bytes 294920 | tf_op jit(solution)/shard_map/ppermute | solution.py:16
  55.2 1.0 collective-permute-done.6
  57.1 1.9 collective-permute-start.7
  59.0 4.3 %collective-permute-start.8 = (f32[3,1,64,128]{3,2,1,0:T(8,128)S(1)}, f32[3,1,64,128]{3,2,1,0:T(8,128)S(1)}, u32[]{:S(2)}, u32[]{:S(2)}) collective-permute-start(f32[3,1,64,128]{3,2,1,0:T(8,128)S(1)} %get-tuple-element.69), channel_id=1, source_target_pairs={{0,1},{1,2},{2,3},{3,4},{4,5},{5,6},{6,7},{8,9},{9,10},{10,11},{11... | collective-permute-start | bytes 294920 | tf_op jit(solution)/shard_map/ppermute | solution.py:16
  65.8 1.9 collective-permute-start.14
  67.8 4.3 %collective-permute-start.15 = (f32[3,1,64,128]{3,2,1,0:T(8,128)S(1)}, f32[3,1,64,128]{3,2,1,0:T(8,128)S(1)}, u32[]{:S(2)}, u32[]{:S(2)}) collective-permute-start(f32[3,1,64,128]{3,2,1,0:T(8,128)S(1)} %get-tuple-element.63), channel_id=1, source_target_pairs={{0,1},{1,2},{2,3},{3,4},{4,5},{5,6},{6,7},{8,9},{9,10},{10,11},{11... | collective-permute-start | bytes 294920 | tf_op jit(solution)/shard_map/ppermute | solution.py:16
  72.4 1.3 collective-permute-done.15
  74.5 1.9 collective-permute-start.16
  76.5 4.3 %collective-permute-start.17 = (f32[3,1,64,128]{3,2,1,0:T(8,128)S(1)}, f32[3,1,64,128]{3,2,1,0:T(8,128)S(1)}, u32[]{:S(2)}, u32[]{:S(2)}) collective-permute-start(f32[3,1,64,128]{3,2,1,0:T(8,128)S(1)} %get-tuple-element.61), channel_id=1, source_target_pairs={{0,1},{1,2},{2,3},{3,4},{4,5},{5,6},{6,7},{8,9},{9,10},{10,11},{11... | collective-permute-start | bytes 294920 | tf_op jit(solution)/shard_map/ppermute | solution.py:16
  81.1 1.3 collective-permute-done.17
  83.3 1.1 collective-permute-start.18
  84.5 1.9 collective-permute-start.10
  86.4 4.6 %collective-permute-start.11 = (f32[3,1,64,128]{3,2,1,0:T(8,128)S(1)}, f32[3,1,64,128]{3,2,1,0:T(8,128)S(1)}, u32[]{:S(2)}, u32[]{:S(2)}) collective-permute-start(f32[3,1,64,128]{3,2,1,0:T(8,128)S(1)} %get-tuple-element.67), channel_id=1, source_target_pairs={{0,1},{1,2},{2,3},{3,4},{4,5},{5,6},{6,7},{8,9},{9,10},{10,11},{11... | collective-permute-start | bytes 294920 | tf_op jit(solution)/shard_map/ppermute | solution.py:16
  91.0 17.9 %collective-permute-done.18 = f32[3,12,64,128]{3,2,1,0:T(8,128)S(1)} collective-permute-done((f32[3,12,64,128]{3,2,1,0:T(8,128)S(1)}, f32[3,12,64,128]{3,2,1,0:T(8,128)S(1)}, u32[]{:S(2)}, u32[]{:S(2)}) %collective-permute-start.18) | collective-permute-done | bytes 1179680 | tf_op jit(solution)/shard_map/ppermute | solution.py:25
  108.9 1.9 collective-permute-start.19
  110.8 5.9 %collective-permute-start.20 = (f32[3,1,64,128]{3,2,1,0:T(8,128)S(1)}, f32[3,1,64,128]{3,2,1,0:T(8,128)S(1)}, u32[]{:S(2)}, u32[]{:S(2)}) collective-permute-start(f32[3,1,64,128]{3,2,1,0:T(8,128)S(1)} %get-tuple-element.59), channel_id=1, source_target_pairs={{0,1},{1,2},{2,3},{3,4},{4,5},{5,6},{6,7},{8,9},{9,10},{10,11},{11... | collective-permute-start | bytes 294920 | tf_op jit(solution)/shard_map/ppermute | solution.py:16
  117.1 1.3 collective-permute-done.20
  119.2 1.9 collective-permute-start.21
  121.1 4.3 %collective-permute-start.22 = (f32[3,1,64,128]{3,2,1,0:T(8,128)S(1)}, f32[3,1,64,128]{3,2,1,0:T(8,128)S(1)}, u32[]{:S(2)}, u32[]{:S(2)}) collective-permute-start(f32[3,1,64,128]{3,2,1,0:T(8,128)S(1)} %get-tuple-element.57), channel_id=1, source_target_pairs={{0,1},{1,2},{2,3},{3,4},{4,5},{5,6},{6,7},{8,9},{9,10},{10,11},{11... | collective-permute-start | bytes 294920 | tf_op jit(solution)/shard_map/ppermute | solution.py:16
  126.4 1.9 collective-permute-start.12
  128.4 3.6 %collective-permute-start.13 = (f32[3,1,64,128]{3,2,1,0:T(8,128)S(1)}, f32[3,1,64,128]{3,2,1,0:T(8,128)S(1)}, u32[]{:S(2)}, u32[]{:S(2)}) collective-permute-start(f32[3,1,64,128]{3,2,1,0:T(8,128)S(1)} %get-tuple-element.65), channel_id=1, source_target_pairs={{0,1},{1,2},{2,3},{3,4},{4,5},{5,6},{6,7},{8,9},{9,10},{10,11},{11... | collective-permute-start | bytes 294920 | tf_op jit(solution)/shard_map/ppermute | solution.py:16
  132.4 1.3 collective-permute-done.13
  133.6 2.5 fusion.41
  136.1 2.0 collective-permute-start.23
  138.2 24.6 %collective-permute-done.23 = f32[3,12,64,128]{3,2,1,0:T(8,128)S(1)} collective-permute-done((f32[3,12,64,128]{3,2,1,0:T(8,128)S(1)}, f32[3,12,64,128]{3,2,1,0:T(8,128)S(1)}, u32[]{:S(2)}, u32[]{:S(2)}) %collective-permute-start.23) | collective-permute-done | bytes 1179680 | tf_op jit(solution)/shard_map/ppermute | solution.py:25
  162.8 1.9 collective-permute-start.24
  164.7 5.7 %collective-permute-start.25 = (f32[3,1,64,128]{3,2,1,0:T(8,128)S(1)}, f32[3,1,64,128]{3,2,1,0:T(8,128)S(1)}, u32[]{:S(2)}, u32[]{:S(2)}) collective-permute-start(f32[3,1,64,128]{3,2,1,0:T(8,128)S(1)} %get-tuple-element.55), channel_id=1, source_target_pairs={{0,1},{1,2},{2,3},{3,4},{4,5},{5,6},{6,7},{8,9},{9,10},{10,11},{11... | collective-permute-start | bytes 294920 | tf_op jit(solution)/shard_map/ppermute | solution.py:16
  170.6 1.3 collective-permute-done.25
  172.5 1.9 collective-permute-start.26
  174.5 4.3 %collective-permute-start.27 = (f32[3,1,64,128]{3,2,1,0:T(8,128)S(1)}, f32[3,1,64,128]{3,2,1,0:T(8,128)S(1)}, u32[]{:S(2)}, u32[]{:S(2)}) collective-permute-start(f32[3,1,64,128]{3,2,1,0:T(8,128)S(1)} %get-tuple-element.53), channel_id=1, source_target_pairs={{0,1},{1,2},{2,3},{3,4},{4,5},{5,6},{6,7},{8,9},{9,10},{10,11},{11... | collective-permute-start | bytes 294920 | tf_op jit(solution)/shard_map/ppermute | solution.py:16
  179.2 1.3 collective-permute-done.27
  181.3 2.4 collective-permute-start.28
  183.6 23.9 %collective-permute-done.28 = f32[3,12,64,128]{3,2,1,0:T(8,128)S(1)} collective-permute-done((f32[3,12,64,128]{3,2,1,0:T(8,128)S(1)}, f32[3,12,64,128]{3,2,1,0:T(8,128)S(1)}, u32[]{:S(2)}, u32[]{:S(2)}) %collective-permute-start.28) | collective-permute-done | bytes 1179680 | tf_op jit(solution)/shard_map/ppermute | solution.py:25
  207.5 1.9 collective-permute-start.29
  209.4 5.0 %collective-permute-start.30 = (f32[3,1,64,128]{3,2,1,0:T(8,128)S(1)}, f32[3,1,64,128]{3,2,1,0:T(8,128)S(1)}, u32[]{:S(2)}, u32[]{:S(2)}) collective-permute-start(f32[3,1,64,128]{3,2,1,0:T(8,128)S(1)} %get-tuple-element.51), channel_id=1, source_target_pairs={{0,1},{1,2},{2,3},{3,4},{4,5},{5,6},{6,7},{8,9},{9,10},{10,11},{11... | collective-permute-start | bytes 294920 | tf_op jit(solution)/shard_map/ppermute | solution.py:16
  214.8 1.3 collective-permute-done.30
  216.8 1.9 collective-permute-start.31
  218.7 4.3 %collective-permute-start.32 = (f32[3,1,64,128]{3,2,1,0:T(8,128)S(1)}, f32[3,1,64,128]{3,2,1,0:T(8,128)S(1)}, u32[]{:S(2)}, u32[]{:S(2)}) collective-permute-start(f32[3,1,64,128]{3,2,1,0:T(8,128)S(1)} %get-tuple-element.49), channel_id=1, source_target_pairs={{0,1},{1,2},{2,3},{3,4},{4,5},{5,6},{6,7},{8,9},{9,10},{10,11},{11... | collective-permute-start | bytes 294920 | tf_op jit(solution)/shard_map/ppermute | solution.py:16
  223.4 1.3 collective-permute-done.32
  225.5 2.4 collective-permute-start.33
  227.8 23.9 %collective-permute-done.33 = f32[3,12,64,128]{3,2,1,0:T(8,128)S(1)} collective-permute-done((f32[3,12,64,128]{3,2,1,0:T(8,128)S(1)}, f32[3,12,64,128]{3,2,1,0:T(8,128)S(1)}, u32[]{:S(2)}, u32[]{:S(2)}) %collective-permute-start.33) | collective-permute-done | bytes 1179680 | tf_op jit(solution)/shard_map/ppermute | solution.py:25
  251.7 1.9 collective-permute-start.34
  253.7 5.0 %collective-permute-start.35 = (f32[3,1,64,128]{3,2,1,0:T(8,128)S(1)}, f32[3,1,64,128]{3,2,1,0:T(8,128)S(1)}, u32[]{:S(2)}, u32[]{:S(2)}) collective-permute-start(f32[3,1,64,128]{3,2,1,0:T(8,128)S(1)} %get-tuple-element.47), channel_id=1, source_target_pairs={{0,1},{1,2},{2,3},{3,4},{4,5},{5,6},{6,7},{8,9},{9,10},{10,11},{11... | collective-permute-start | bytes 294920 | tf_op jit(solution)/shard_map/ppermute | solution.py:16
  259.0 1.3 collective-permute-done.35
  261.0 1.9 collective-permute-start.36
  262.9 4.3 %collective-permute-start.37 = (f32[3,1,64,128]{3,2,1,0:T(8,128)S(1)}, f32[3,1,64,128]{3,2,1,0:T(8,128)S(1)}, u32[]{:S(2)}, u32[]{:S(2)}) collective-permute-start(f32[3,1,64,128]{3,2,1,0:T(8,128)S(1)} %get-tuple-element.45), channel_id=1, source_target_pairs={{0,1},{1,2},{2,3},{3,4},{4,5},{5,6},{6,7},{8,9},{9,10},{10,11},{11... | collective-permute-start | bytes 294920 | tf_op jit(solution)/shard_map/ppermute | solution.py:16
  267.6 1.3 collective-permute-done.37
  268.9 1.0 multiply_reduce_fusion.1
  269.9 1.9 collective-permute-start.38
  271.9 4.3 %collective-permute-start.39 = (f32[3,1,64,128]{3,2,1,0:T(8,128)S(1)}, f32[3,1,64,128]{3,2,1,0:T(8,128)S(1)}, u32[]{:S(2)}, u32[]{:S(2)}) collective-permute-start(f32[3,1,64,128]{3,2,1,0:T(8,128)S(1)} %get-tuple-element.43), channel_id=1, source_target_pairs={{0,1},{1,2},{2,3},{3,4},{4,5},{5,6},{6,7},{8,9},{9,10},{10,11},{11... | collective-permute-start | bytes 294920 | tf_op jit(solution)/shard_map/ppermute | solution.py:16
  276.5 1.3 collective-permute-done.39
  278.6 1.9 collective-permute-start.40
  280.6 4.3 %collective-permute-start.41 = (f32[3,1,64,128]{3,2,1,0:T(8,128)S(1)}, f32[3,1,64,128]{3,2,1,0:T(8,128)S(1)}, u32[]{:S(2)}, u32[]{:S(2)}) collective-permute-start(f32[3,1,64,128]{3,2,1,0:T(8,128)S(1)} %get-tuple-element.41), channel_id=1, source_target_pairs={{0,1},{1,2},{2,3},{3,4},{4,5},{5,6},{6,7},{8,9},{9,10},{10,11},{11... | collective-permute-start | bytes 294920 | tf_op jit(solution)/shard_map/ppermute | solution.py:16
  285.2 1.3 collective-permute-done.41
  287.3 1.7 pad_maximum_fusion
  (84 shorter events, 21.3 us)
Async XLA Ops:
  0.6 7.4 %copy-start.2 = (f32[2,3,12,64,128]{4,3,2,1,0:T(8,128)S(1)}, f32[2,3,12,64,128]{4,3,2,1,0:T(8,128)}, u32[]{:S(2)}) copy-start(f32[2,3,12,64,128]{4,3,2,1,0:T(8,128)} %param.5) | copy-start | bytes 7077892
  2.2 6.0 %copy-start.3 = (s32[12,64,128]{2,1,0:T(8,128)S(1)}, s32[12,64,128]{2,1,0:T(8,128)}, u32[]{:S(2)}) copy-start(s32[12,64,128]{2,1,0:T(8,128)} %param.7) | copy-start | bytes 1179652
  2.2 6.0 %copy-start.4 = (f32[4]{0:T(128)S(1)}, f32[4]{0:T(128)}, u32[]{:S(2)}) copy-start(f32[4]{0:T(128)} %param.9) | copy-start | bytes 52
  2.2 6.0 %copy-start.5 = (f32[4]{0:T(128)S(1)}, f32[4]{0:T(128)}, u32[]{:S(2)}) copy-start(f32[4]{0:T(128)} %param.8) | copy-start | bytes 52
  2.2 6.5 %collective-permute-start = (f32[3,1,64,128]{3,2,1,0:T(8,128)S(1)}, f32[3,1,64,128]{3,2,1,0:T(8,128)S(1)}, u32[]{:S(2)}, u32[]{:S(2)}) collective-permute-start(f32[3,1,64,128]{3,2,1,0:T(8,128)S(1)} %get-tuple-element.74), channel_id=1, source_target_pairs={{1,0},{2,1},{3,2},{4,3},{5,4},{6,5},{7,6},{9,8},{10,9},{11,10},{12... | collective-permute-start | bytes 294920 | tf_op jit(solution)/shard_map/ppermute | solution.py:17
  5.0 4.7 %collective-permute-start.1 = (f32[3,1,64,128]{3,2,1,0:T(8,128)S(1)}, f32[3,1,64,128]{3,2,1,0:T(8,128)S(1)}, u32[]{:S(2)}, u32[]{:S(2)}) collective-permute-start(f32[3,1,64,128]{3,2,1,0:T(8,128)S(1)} %get-tuple-element.75), channel_id=1, source_target_pairs={{0,1},{1,2},{2,3},{3,4},{4,5},{5,6},{6,7},{8,9},{9,10},{10,11},{11... | collective-permute-start | bytes 294920 | tf_op jit(solution)/shard_map/ppermute | solution.py:16
  8.2 1.7 copy-start
  10.8 6.4 %collective-permute-start.2 = (f32[3,1,64,128]{3,2,1,0:T(8,128)S(1)}, f32[3,1,64,128]{3,2,1,0:T(8,128)S(1)}, u32[]{:S(2)}, u32[]{:S(2)}) collective-permute-start(f32[3,1,64,128]{3,2,1,0:T(8,128)S(1)} %get-tuple-element.72), channel_id=1, source_target_pairs={{1,0},{2,1},{3,2},{4,3},{5,4},{6,5},{7,6},{9,8},{10,9},{11,10},{12... | collective-permute-start | bytes 294920 | tf_op jit(solution)/shard_map/ppermute | solution.py:17
  12.7 5.7 %collective-permute-start.3 = (f32[3,1,64,128]{3,2,1,0:T(8,128)S(1)}, f32[3,1,64,128]{3,2,1,0:T(8,128)S(1)}, u32[]{:S(2)}, u32[]{:S(2)}) collective-permute-start(f32[3,1,64,128]{3,2,1,0:T(8,128)S(1)} %get-tuple-element.73), channel_id=1, source_target_pairs={{0,1},{1,2},{2,3},{3,4},{4,5},{5,6},{6,7},{8,9},{9,10},{10,11},{11... | collective-permute-start | bytes 294920 | tf_op jit(solution)/shard_map/ppermute | solution.py:16
  19.3 28.1 %collective-permute-start.4 = (f32[3,12,64,128]{3,2,1,0:T(8,128)S(1)}, f32[3,12,64,128]{3,2,1,0:T(8,128)S(1)}, u32[]{:S(2)}, u32[]{:S(2)}) collective-permute-start(f32[3,12,64,128]{3,2,1,0:T(8,128)S(1)} %fusion.12), channel_id=1, source_target_pairs={{24,0},{0,8},{8,16},{16,24},{25,1},{1,9},{9,17},{17,25},{26,2},{2,... | collective-permute-start | bytes 3538952 | tf_op jit(solution)/shard_map/ppermute | solution.py:25
  19.7 64.7 %collective-permute-start.9 = (f32[3,12,64,128]{3,2,1,0:T(8,128)S(1)}, f32[3,12,64,128]{3,2,1,0:T(8,128)S(1)}, u32[]{:S(2)}, u32[]{:S(2)}) collective-permute-start(f32[3,12,64,128]{3,2,1,0:T(8,128)S(1)} %broadcast_in_dim.25), channel_id=1, source_target_pairs={{24,0},{0,8},{8,16},{16,24},{25,1},{1,9},{9,17},{17,25},{26,2},{2,... | collective-permute-start | bytes 3538952 | tf_op jit(solution)/shard_map/ppermute | solution.py:25
  47.5 7.8 %collective-permute-start.5 = (f32[3,1,64,128]{3,2,1,0:T(8,128)S(1)}, f32[3,1,64,128]{3,2,1,0:T(8,128)S(1)}, u32[]{:S(2)}, u32[]{:S(2)}) collective-permute-start(f32[3,1,64,128]{3,2,1,0:T(8,128)S(1)} %get-tuple-element.70), channel_id=1, source_target_pairs={{1,0},{2,1},{3,2},{4,3},{5,4},{6,5},{7,6},{9,8},{10,9},{11,10},{12... | collective-permute-start | bytes 294920 | tf_op jit(solution)/shard_map/ppermute | solution.py:17
  49.4 6.8 %collective-permute-start.6 = (f32[3,1,64,128]{3,2,1,0:T(8,128)S(1)}, f32[3,1,64,128]{3,2,1,0:T(8,128)S(1)}, u32[]{:S(2)}, u32[]{:S(2)}) collective-permute-start(f32[3,1,64,128]{3,2,1,0:T(8,128)S(1)} %get-tuple-element.71), channel_id=1, source_target_pairs={{0,1},{1,2},{2,3},{3,4},{4,5},{5,6},{6,7},{8,9},{9,10},{10,11},{11... | collective-permute-start | bytes 294920 | tf_op jit(solution)/shard_map/ppermute | solution.py:16
  57.1 6.9 %collective-permute-start.7 = (f32[3,1,64,128]{3,2,1,0:T(8,128)S(1)}, f32[3,1,64,128]{3,2,1,0:T(8,128)S(1)}, u32[]{:S(2)}, u32[]{:S(2)}) collective-permute-start(f32[3,1,64,128]{3,2,1,0:T(8,128)S(1)} %get-tuple-element.68), channel_id=1, source_target_pairs={{1,0},{2,1},{3,2},{4,3},{5,4},{6,5},{7,6},{9,8},{10,9},{11,10},{12... | collective-permute-start | bytes 294920 | tf_op jit(solution)/shard_map/ppermute | solution.py:17
  59.0 5.9 %collective-permute-start.8 = (f32[3,1,64,128]{3,2,1,0:T(8,128)S(1)}, f32[3,1,64,128]{3,2,1,0:T(8,128)S(1)}, u32[]{:S(2)}, u32[]{:S(2)}) collective-permute-start(f32[3,1,64,128]{3,2,1,0:T(8,128)S(1)} %get-tuple-element.69), channel_id=1, source_target_pairs={{0,1},{1,2},{2,3},{3,4},{4,5},{5,6},{6,7},{8,9},{9,10},{10,11},{11... | collective-permute-start | bytes 294920 | tf_op jit(solution)/shard_map/ppermute | solution.py:16
  65.8 6.6 %collective-permute-start.14 = (f32[3,1,64,128]{3,2,1,0:T(8,128)S(1)}, f32[3,1,64,128]{3,2,1,0:T(8,128)S(1)}, u32[]{:S(2)}, u32[]{:S(2)}) collective-permute-start(f32[3,1,64,128]{3,2,1,0:T(8,128)S(1)} %get-tuple-element.62), channel_id=1, source_target_pairs={{1,0},{2,1},{3,2},{4,3},{5,4},{6,5},{7,6},{9,8},{10,9},{11,10},{12... | collective-permute-start | bytes 294920 | tf_op jit(solution)/shard_map/ppermute | solution.py:17
  67.8 5.9 %collective-permute-start.15 = (f32[3,1,64,128]{3,2,1,0:T(8,128)S(1)}, f32[3,1,64,128]{3,2,1,0:T(8,128)S(1)}, u32[]{:S(2)}, u32[]{:S(2)}) collective-permute-start(f32[3,1,64,128]{3,2,1,0:T(8,128)S(1)} %get-tuple-element.63), channel_id=1, source_target_pairs={{0,1},{1,2},{2,3},{3,4},{4,5},{5,6},{6,7},{8,9},{9,10},{10,11},{11... | collective-permute-start | bytes 294920 | tf_op jit(solution)/shard_map/ppermute | solution.py:16
  74.5 6.6 %collective-permute-start.16 = (f32[3,1,64,128]{3,2,1,0:T(8,128)S(1)}, f32[3,1,64,128]{3,2,1,0:T(8,128)S(1)}, u32[]{:S(2)}, u32[]{:S(2)}) collective-permute-start(f32[3,1,64,128]{3,2,1,0:T(8,128)S(1)} %get-tuple-element.60), channel_id=1, source_target_pairs={{1,0},{2,1},{3,2},{4,3},{5,4},{6,5},{7,6},{9,8},{10,9},{11,10},{12... | collective-permute-start | bytes 294920 | tf_op jit(solution)/shard_map/ppermute | solution.py:17
  76.5 5.9 %collective-permute-start.17 = (f32[3,1,64,128]{3,2,1,0:T(8,128)S(1)}, f32[3,1,64,128]{3,2,1,0:T(8,128)S(1)}, u32[]{:S(2)}, u32[]{:S(2)}) collective-permute-start(f32[3,1,64,128]{3,2,1,0:T(8,128)S(1)} %get-tuple-element.61), channel_id=1, source_target_pairs={{0,1},{1,2},{2,3},{3,4},{4,5},{5,6},{6,7},{8,9},{9,10},{10,11},{11... | collective-permute-start | bytes 294920 | tf_op jit(solution)/shard_map/ppermute | solution.py:16
  83.3 25.6 %collective-permute-start.18 = (f32[3,12,64,128]{3,2,1,0:T(8,128)S(1)}, f32[3,12,64,128]{3,2,1,0:T(8,128)S(1)}, u32[]{:S(2)}, u32[]{:S(2)}) collective-permute-start(f32[3,12,64,128]{3,2,1,0:T(8,128)S(1)} %fusion.55), channel_id=1, source_target_pairs={{24,0},{0,8},{8,16},{16,24},{25,1},{1,9},{9,17},{17,25},{26,2},{2,... | collective-permute-start | bytes 3538952 | tf_op jit(solution)/shard_map/ppermute | solution.py:25
  84.5 41.2 %collective-permute-start.10 = (f32[3,1,64,128]{3,2,1,0:T(8,128)S(1)}, f32[3,1,64,128]{3,2,1,0:T(8,128)S(1)}, u32[]{:S(2)}, u32[]{:S(2)}) collective-permute-start(f32[3,1,64,128]{3,2,1,0:T(8,128)S(1)} %get-tuple-element.66), channel_id=1, source_target_pairs={{1,0},{2,1},{3,2},{4,3},{5,4},{6,5},{7,6},{9,8},{10,9},{11,10},{12... | collective-permute-start | bytes 294920 | tf_op jit(solution)/shard_map/ppermute | solution.py:17
  86.4 39.3 %collective-permute-start.11 = (f32[3,1,64,128]{3,2,1,0:T(8,128)S(1)}, f32[3,1,64,128]{3,2,1,0:T(8,128)S(1)}, u32[]{:S(2)}, u32[]{:S(2)}) collective-permute-start(f32[3,1,64,128]{3,2,1,0:T(8,128)S(1)} %get-tuple-element.67), channel_id=1, source_target_pairs={{0,1},{1,2},{2,3},{3,4},{4,5},{5,6},{6,7},{8,9},{9,10},{10,11},{11... | collective-permute-start | bytes 294920 | tf_op jit(solution)/shard_map/ppermute | solution.py:16
  108.9 8.2 %collective-permute-start.19 = (f32[3,1,64,128]{3,2,1,0:T(8,128)S(1)}, f32[3,1,64,128]{3,2,1,0:T(8,128)S(1)}, u32[]{:S(2)}, u32[]{:S(2)}) collective-permute-start(f32[3,1,64,128]{3,2,1,0:T(8,128)S(1)} %get-tuple-element.58), channel_id=1, source_target_pairs={{1,0},{2,1},{3,2},{4,3},{5,4},{6,5},{7,6},{9,8},{10,9},{11,10},{12... | collective-permute-start | bytes 294920 | tf_op jit(solution)/shard_map/ppermute | solution.py:17
  110.8 7.5 %collective-permute-start.20 = (f32[3,1,64,128]{3,2,1,0:T(8,128)S(1)}, f32[3,1,64,128]{3,2,1,0:T(8,128)S(1)}, u32[]{:S(2)}, u32[]{:S(2)}) collective-permute-start(f32[3,1,64,128]{3,2,1,0:T(8,128)S(1)} %get-tuple-element.59), channel_id=1, source_target_pairs={{0,1},{1,2},{2,3},{3,4},{4,5},{5,6},{6,7},{8,9},{9,10},{10,11},{11... | collective-permute-start | bytes 294920 | tf_op jit(solution)/shard_map/ppermute | solution.py:16
  119.2 12.8 %collective-permute-start.21 = (f32[3,1,64,128]{3,2,1,0:T(8,128)S(1)}, f32[3,1,64,128]{3,2,1,0:T(8,128)S(1)}, u32[]{:S(2)}, u32[]{:S(2)}) collective-permute-start(f32[3,1,64,128]{3,2,1,0:T(8,128)S(1)} %get-tuple-element.56), channel_id=1, source_target_pairs={{1,0},{2,1},{3,2},{4,3},{5,4},{6,5},{7,6},{9,8},{10,9},{11,10},{12... | collective-permute-start | bytes 294920 | tf_op jit(solution)/shard_map/ppermute | solution.py:17
  121.1 10.9 %collective-permute-start.22 = (f32[3,1,64,128]{3,2,1,0:T(8,128)S(1)}, f32[3,1,64,128]{3,2,1,0:T(8,128)S(1)}, u32[]{:S(2)}, u32[]{:S(2)}) collective-permute-start(f32[3,1,64,128]{3,2,1,0:T(8,128)S(1)} %get-tuple-element.57), channel_id=1, source_target_pairs={{0,1},{1,2},{2,3},{3,4},{4,5},{5,6},{6,7},{8,9},{9,10},{10,11},{11... | collective-permute-start | bytes 294920 | tf_op jit(solution)/shard_map/ppermute | solution.py:16
  126.4 5.9 %collective-permute-start.12 = (f32[3,1,64,128]{3,2,1,0:T(8,128)S(1)}, f32[3,1,64,128]{3,2,1,0:T(8,128)S(1)}, u32[]{:S(2)}, u32[]{:S(2)}) collective-permute-start(f32[3,1,64,128]{3,2,1,0:T(8,128)S(1)} %get-tuple-element.64), channel_id=1, source_target_pairs={{1,0},{2,1},{3,2},{4,3},{5,4},{6,5},{7,6},{9,8},{10,9},{11,10},{12... | collective-permute-start | bytes 294920 | tf_op jit(solution)/shard_map/ppermute | solution.py:17
  128.4 5.3 %collective-permute-start.13 = (f32[3,1,64,128]{3,2,1,0:T(8,128)S(1)}, f32[3,1,64,128]{3,2,1,0:T(8,128)S(1)}, u32[]{:S(2)}, u32[]{:S(2)}) collective-permute-start(f32[3,1,64,128]{3,2,1,0:T(8,128)S(1)} %get-tuple-element.65), channel_id=1, source_target_pairs={{0,1},{1,2},{2,3},{3,4},{4,5},{5,6},{6,7},{8,9},{9,10},{10,11},{11... | collective-permute-start | bytes 294920 | tf_op jit(solution)/shard_map/ppermute | solution.py:16
  136.1 132.7 %copy-start.1 = (f32[3,12,64,128]{3,2,1,0:T(8,128)}, f32[3,12,64,128]{3,2,1,0:T(8,128)S(1)}, u32[]{:S(2)}) copy-start(f32[3,12,64,128]{3,2,1,0:T(8,128)S(1)} %get-tuple-element.13) | copy-start | bytes 3538948
  136.1 26.6 %collective-permute-start.23 = (f32[3,12,64,128]{3,2,1,0:T(8,128)S(1)}, f32[3,12,64,128]{3,2,1,0:T(8,128)S(1)}, u32[]{:S(2)}, u32[]{:S(2)}) collective-permute-start(f32[3,12,64,128]{3,2,1,0:T(8,128)S(1)} %get-tuple-element.12), channel_id=1, source_target_pairs={{24,0},{0,8},{8,16},{16,24},{25,1},{1,9},{9,17},{17,25},{26,2},{2,... | collective-permute-start | bytes 3538952 | tf_op jit(solution)/shard_map/ppermute | solution.py:25
  162.8 7.8 %collective-permute-start.24 = (f32[3,1,64,128]{3,2,1,0:T(8,128)S(1)}, f32[3,1,64,128]{3,2,1,0:T(8,128)S(1)}, u32[]{:S(2)}, u32[]{:S(2)}) collective-permute-start(f32[3,1,64,128]{3,2,1,0:T(8,128)S(1)} %get-tuple-element.54), channel_id=1, source_target_pairs={{1,0},{2,1},{3,2},{4,3},{5,4},{6,5},{7,6},{9,8},{10,9},{11,10},{12... | collective-permute-start | bytes 294920 | tf_op jit(solution)/shard_map/ppermute | solution.py:17
  164.7 7.1 %collective-permute-start.25 = (f32[3,1,64,128]{3,2,1,0:T(8,128)S(1)}, f32[3,1,64,128]{3,2,1,0:T(8,128)S(1)}, u32[]{:S(2)}, u32[]{:S(2)}) collective-permute-start(f32[3,1,64,128]{3,2,1,0:T(8,128)S(1)} %get-tuple-element.55), channel_id=1, source_target_pairs={{0,1},{1,2},{2,3},{3,4},{4,5},{5,6},{6,7},{8,9},{9,10},{10,11},{11... | collective-permute-start | bytes 294920 | tf_op jit(solution)/shard_map/ppermute | solution.py:16
  172.5 6.6 %collective-permute-start.26 = (f32[3,1,64,128]{3,2,1,0:T(8,128)S(1)}, f32[3,1,64,128]{3,2,1,0:T(8,128)S(1)}, u32[]{:S(2)}, u32[]{:S(2)}) collective-permute-start(f32[3,1,64,128]{3,2,1,0:T(8,128)S(1)} %get-tuple-element.52), channel_id=1, source_target_pairs={{1,0},{2,1},{3,2},{4,3},{5,4},{6,5},{7,6},{9,8},{10,9},{11,10},{12... | collective-permute-start | bytes 294920 | tf_op jit(solution)/shard_map/ppermute | solution.py:17
  174.5 5.9 %collective-permute-start.27 = (f32[3,1,64,128]{3,2,1,0:T(8,128)S(1)}, f32[3,1,64,128]{3,2,1,0:T(8,128)S(1)}, u32[]{:S(2)}, u32[]{:S(2)}) collective-permute-start(f32[3,1,64,128]{3,2,1,0:T(8,128)S(1)} %get-tuple-element.53), channel_id=1, source_target_pairs={{0,1},{1,2},{2,3},{3,4},{4,5},{5,6},{6,7},{8,9},{9,10},{10,11},{11... | collective-permute-start | bytes 294920 | tf_op jit(solution)/shard_map/ppermute | solution.py:16
  181.3 26.2 %collective-permute-start.28 = (f32[3,12,64,128]{3,2,1,0:T(8,128)S(1)}, f32[3,12,64,128]{3,2,1,0:T(8,128)S(1)}, u32[]{:S(2)}, u32[]{:S(2)}) collective-permute-start(f32[3,12,64,128]{3,2,1,0:T(8,128)S(1)} %fusion.85), channel_id=1, source_target_pairs={{24,0},{0,8},{8,16},{16,24},{25,1},{1,9},{9,17},{17,25},{26,2},{2,... | collective-permute-start | bytes 3538952 | tf_op jit(solution)/shard_map/ppermute | solution.py:25
  207.5 7.3 %collective-permute-start.29 = (f32[3,1,64,128]{3,2,1,0:T(8,128)S(1)}, f32[3,1,64,128]{3,2,1,0:T(8,128)S(1)}, u32[]{:S(2)}, u32[]{:S(2)}) collective-permute-start(f32[3,1,64,128]{3,2,1,0:T(8,128)S(1)} %get-tuple-element.50), channel_id=1, source_target_pairs={{1,0},{2,1},{3,2},{4,3},{5,4},{6,5},{7,6},{9,8},{10,9},{11,10},{12... | collective-permute-start | bytes 294920 | tf_op jit(solution)/shard_map/ppermute | solution.py:17
  209.4 6.6 %collective-permute-start.30 = (f32[3,1,64,128]{3,2,1,0:T(8,128)S(1)}, f32[3,1,64,128]{3,2,1,0:T(8,128)S(1)}, u32[]{:S(2)}, u32[]{:S(2)}) collective-permute-start(f32[3,1,64,128]{3,2,1,0:T(8,128)S(1)} %get-tuple-element.51), channel_id=1, source_target_pairs={{0,1},{1,2},{2,3},{3,4},{4,5},{5,6},{6,7},{8,9},{9,10},{10,11},{11... | collective-permute-start | bytes 294920 | tf_op jit(solution)/shard_map/ppermute | solution.py:16
  216.8 6.6 %collective-permute-start.31 = (f32[3,1,64,128]{3,2,1,0:T(8,128)S(1)}, f32[3,1,64,128]{3,2,1,0:T(8,128)S(1)}, u32[]{:S(2)}, u32[]{:S(2)}) collective-permute-start(f32[3,1,64,128]{3,2,1,0:T(8,128)S(1)} %get-tuple-element.48), channel_id=1, source_target_pairs={{1,0},{2,1},{3,2},{4,3},{5,4},{6,5},{7,6},{9,8},{10,9},{11,10},{12... | collective-permute-start | bytes 294920 | tf_op jit(solution)/shard_map/ppermute | solution.py:17
  218.7 5.9 %collective-permute-start.32 = (f32[3,1,64,128]{3,2,1,0:T(8,128)S(1)}, f32[3,1,64,128]{3,2,1,0:T(8,128)S(1)}, u32[]{:S(2)}, u32[]{:S(2)}) collective-permute-start(f32[3,1,64,128]{3,2,1,0:T(8,128)S(1)} %get-tuple-element.49), channel_id=1, source_target_pairs={{0,1},{1,2},{2,3},{3,4},{4,5},{5,6},{6,7},{8,9},{9,10},{10,11},{11... | collective-permute-start | bytes 294920 | tf_op jit(solution)/shard_map/ppermute | solution.py:16
  225.5 26.2 %collective-permute-start.33 = (f32[3,12,64,128]{3,2,1,0:T(8,128)S(1)}, f32[3,12,64,128]{3,2,1,0:T(8,128)S(1)}, u32[]{:S(2)}, u32[]{:S(2)}) collective-permute-start(f32[3,12,64,128]{3,2,1,0:T(8,128)S(1)} %fusion.100), channel_id=1, source_target_pairs={{24,0},{0,8},{8,16},{16,24},{25,1},{1,9},{9,17},{17,25},{26,2},{2,... | collective-permute-start | bytes 3538952 | tf_op jit(solution)/shard_map/ppermute | solution.py:25
  251.7 7.3 %collective-permute-start.34 = (f32[3,1,64,128]{3,2,1,0:T(8,128)S(1)}, f32[3,1,64,128]{3,2,1,0:T(8,128)S(1)}, u32[]{:S(2)}, u32[]{:S(2)}) collective-permute-start(f32[3,1,64,128]{3,2,1,0:T(8,128)S(1)} %get-tuple-element.46), channel_id=1, source_target_pairs={{1,0},{2,1},{3,2},{4,3},{5,4},{6,5},{7,6},{9,8},{10,9},{11,10},{12... | collective-permute-start | bytes 294920 | tf_op jit(solution)/shard_map/ppermute | solution.py:17
  253.7 6.6 %collective-permute-start.35 = (f32[3,1,64,128]{3,2,1,0:T(8,128)S(1)}, f32[3,1,64,128]{3,2,1,0:T(8,128)S(1)}, u32[]{:S(2)}, u32[]{:S(2)}) collective-permute-start(f32[3,1,64,128]{3,2,1,0:T(8,128)S(1)} %get-tuple-element.47), channel_id=1, source_target_pairs={{0,1},{1,2},{2,3},{3,4},{4,5},{5,6},{6,7},{8,9},{9,10},{10,11},{11... | collective-permute-start | bytes 294920 | tf_op jit(solution)/shard_map/ppermute | solution.py:16
  261.0 6.6 %collective-permute-start.36 = (f32[3,1,64,128]{3,2,1,0:T(8,128)S(1)}, f32[3,1,64,128]{3,2,1,0:T(8,128)S(1)}, u32[]{:S(2)}, u32[]{:S(2)}) collective-permute-start(f32[3,1,64,128]{3,2,1,0:T(8,128)S(1)} %get-tuple-element.44), channel_id=1, source_target_pairs={{1,0},{2,1},{3,2},{4,3},{5,4},{6,5},{7,6},{9,8},{10,9},{11,10},{12... | collective-permute-start | bytes 294920 | tf_op jit(solution)/shard_map/ppermute | solution.py:17
  262.9 5.9 %collective-permute-start.37 = (f32[3,1,64,128]{3,2,1,0:T(8,128)S(1)}, f32[3,1,64,128]{3,2,1,0:T(8,128)S(1)}, u32[]{:S(2)}, u32[]{:S(2)}) collective-permute-start(f32[3,1,64,128]{3,2,1,0:T(8,128)S(1)} %get-tuple-element.45), channel_id=1, source_target_pairs={{0,1},{1,2},{2,3},{3,4},{4,5},{5,6},{6,7},{8,9},{9,10},{10,11},{11... | collective-permute-start | bytes 294920 | tf_op jit(solution)/shard_map/ppermute | solution.py:16
  269.9 6.6 %collective-permute-start.38 = (f32[3,1,64,128]{3,2,1,0:T(8,128)S(1)}, f32[3,1,64,128]{3,2,1,0:T(8,128)S(1)}, u32[]{:S(2)}, u32[]{:S(2)}) collective-permute-start(f32[3,1,64,128]{3,2,1,0:T(8,128)S(1)} %get-tuple-element.42), channel_id=1, source_target_pairs={{1,0},{2,1},{3,2},{4,3},{5,4},{6,5},{7,6},{9,8},{10,9},{11,10},{12... | collective-permute-start | bytes 294920 | tf_op jit(solution)/shard_map/ppermute | solution.py:17
  271.9 5.9 %collective-permute-start.39 = (f32[3,1,64,128]{3,2,1,0:T(8,128)S(1)}, f32[3,1,64,128]{3,2,1,0:T(8,128)S(1)}, u32[]{:S(2)}, u32[]{:S(2)}) collective-permute-start(f32[3,1,64,128]{3,2,1,0:T(8,128)S(1)} %get-tuple-element.43), channel_id=1, source_target_pairs={{0,1},{1,2},{2,3},{3,4},{4,5},{5,6},{6,7},{8,9},{9,10},{10,11},{11... | collective-permute-start | bytes 294920 | tf_op jit(solution)/shard_map/ppermute | solution.py:16
  278.6 6.6 %collective-permute-start.40 = (f32[3,1,64,128]{3,2,1,0:T(8,128)S(1)}, f32[3,1,64,128]{3,2,1,0:T(8,128)S(1)}, u32[]{:S(2)}, u32[]{:S(2)}) collective-permute-start(f32[3,1,64,128]{3,2,1,0:T(8,128)S(1)} %get-tuple-element.40), channel_id=1, source_target_pairs={{1,0},{2,1},{3,2},{4,3},{5,4},{6,5},{7,6},{9,8},{10,9},{11,10},{12... | collective-permute-start | bytes 294920 | tf_op jit(solution)/shard_map/ppermute | solution.py:17
  280.6 5.9 %collective-permute-start.41 = (f32[3,1,64,128]{3,2,1,0:T(8,128)S(1)}, f32[3,1,64,128]{3,2,1,0:T(8,128)S(1)}, u32[]{:S(2)}, u32[]{:S(2)}) collective-permute-start(f32[3,1,64,128]{3,2,1,0:T(8,128)S(1)} %get-tuple-element.41), channel_id=1, source_target_pairs={{0,1},{1,2},{2,3},{3,4},{4,5},{5,6},{6,7},{8,9},{9,10},{10,11},{11... | collective-permute-start | bytes 294920 | tf_op jit(solution)/shard_map/ppermute | solution.py:16
where the time goes:
time: 293 us; the launch traced here: 289 us
  waiting for transfers between devices  140 us (48%)
  starting transfers between devices  126 us (43%)
  other arithmetic  19.4 us (7%)
    ppermute x6, waiting for transfers between devices, shifted(): return lax.ppermute(block, axis, route)  117 us
    ppermute x18, starting transfers between devices, extended_2(): before = lax.ppermute(last, axis, up)  81 us
    ppermute x18, starting transfers between devices, extended_2(): after = lax.ppermute(leading, axis, down)  35.4 us
    ppermute x18, waiting for transfers between devices, extended_2(): before = lax.ppermute(last, axis, up)  19.3 us
    ppermute x6, starting transfers between devices, shifted(): return lax.ppermute(block, axis, route)  9.42 us
    reduce_sum x10, other arithmetic, fine_update(): square = jnp.sum(centre * centre, axis=0)  6.34 us
  transfers between devices with their start and end apart: 42, of which 36 were waited for; matrix products, arithmetic and copies ran while one was open for 3% of the time, Pallas kernels for 0%

commit v1 on v0

v1 whole, which is shorter than its diff:
```python
import jax
import jax.numpy as jnp
from jax import lax
from jax.experimental import pallas as pl
from jax.experimental.pallas import tpu as pltpu
from jax.sharding import PartitionSpec as P

PICARD = 2
MESH = pl.DeviceIdType.MESH
PAD = 8


def place(index, count):
    if count % 4:
        return index
    odd_pair = lax.rem(lax.div(index, 2), 2)
    return index + odd_pair * (1 - 2 * lax.rem(index, 2))


def neighbour_sum(state, x, layers, r0, rows, halo):
    middle, lanes = pl.ds(PAD + r0, rows), state.shape[-1]
    centre = state[:, pl.ds(x + 1, layers), middle, :]
    first = state[:, pl.ds(x + 2, layers), middle, :] + state[:, pl.ds(x, layers), middle, :]
    above = state[:, pl.ds(x + 1, layers), pl.ds(PAD + r0 - 1, rows), :]
    below = state[:, pl.ds(x + 1, layers), pl.ds(PAD + r0 + 1, rows), :]
    if halo is not None:
        top, bottom, depth = halo
        row = lax.broadcasted_iota(jnp.int32, (rows, lanes), 0)

        def filled(side, values, at):
            return jnp.stack([
                jnp.stack([
                    jnp.where(
                        row == at,
                        jnp.broadcast_to(side[pl.ds(c * depth + x + i, 1), :], (rows, lanes)),
                        values[c, i],
                    )
                    for i in range(layers)
                ])
                for c in range(3)
            ])

        above = filled(top, above, 0)
        below = filled(bottom, below, rows - 1)
    flat = centre.reshape(-1, lanes)
    lane = lax.broadcasted_iota(jnp.int32, flat.shape, 1)
    left = jnp.where(lane == 0, 0.0, pltpu.roll(flat, 1, 1))
    right = jnp.where(lane == lanes - 1, 0.0, pltpu.roll(flat, lanes - 1, 1))
    third = (left + right).reshape(centre.shape)
    return centre, (first + (above + below)) + third


def fine(centre, total, known, cond, nu0):
    s = (centre[0] * centre[0] + centre[1] * centre[1]) + centre[2] * centre[2]
    one = 1.0 + s
    weight = nu0 * (one + 0.5 * s)
    scale = 1.0 / (cond * one + 6.0 * weight)
    return (known * (one * scale)[None]) + (weight * scale)[None] * total


def kernel(
    n_tm, n_space,
    guess, source, regions, conductance, reluct,
    field, residual,
    home, home_force, home_known, home_cond, home_nu,
    state, force0, force1, known, points, res, out0,
    cond, nu0, w_old, w_sum,
    row_out, row_in,
    load_sem, home_send, home_recv, halo_send, halo_recv,
    move_send, move_recv, back_send, back_recv, store_sem,
):
    steps, _, depth, height, lanes = guess.shape
    rows = height // n_tm
    t, s = lax.axis_index("tm"), lax.axis_index("space")
    p = place(t, n_tm)
    lower_x, upper_x = s > 0, s < n_space - 1
    lower_y, upper_y = p > 0, p < n_tm - 1

    def wrap(i):
        return lax.rem(i + n_tm, n_tm)

    def block(index):
        return pl.ds(pl.multiple_of(place(index, n_tm) * rows, 8), rows)

    def home_block(index):
        return pl.ds(pl.multiple_of(place(index, n_tm) * rows + PAD, 8), rows)

    load_guess = pltpu.make_async_copy(
        guess.at[0], home.at[0, :, pl.ds(1, depth), pl.ds(PAD, height), :], load_sem.at[0]
    )
    load_force = pltpu.make_async_copy(source.at[1], home_force, load_sem.at[1])
    load_guess.start()
    load_force.start()

    zero_layer = jnp.zeros((3, height, lanes), jnp.float32)
    for b in range(2):
        home[b, :, 0, pl.ds(PAD, height), :] = zero_layer
        home[b, :, depth + 1, pl.ds(PAD, height), :] = zero_layer
        for r0 in (0, PAD + height):
            home[b, :, :, pl.ds(r0, PAD), :] = jnp.zeros((3, depth + 2, PAD, lanes), jnp.float32)
    for b in range(3):
        for layer in (0, depth + 1):
            state[b, :, :, layer, pl.ds(PAD, rows), :] = jnp.zeros((n_tm, 3, rows, lanes), jnp.float32)
    row_in[...] = jnp.zeros_like(row_in)

    barrier = pltpu.get_barrier_semaphore()
    for i in range(1, n_tm):
        pl.semaphore_signal(barrier, inc=1, device_id=(wrap(t + i), s), device_id_type=MESH)

    @pl.when(lower_x)
    def _():
        pl.semaphore_signal(barrier, inc=1, device_id=(t, s - 1), device_id_type=MESH)

    @pl.when(upper_x)
    def _():
        pl.semaphore_signal(barrier, inc=1, device_id=(t, s + 1), device_id_type=MESH)

    between = jnp.logical_and(lower_x, upper_x)

    @pl.when(between)
    def _():
        pl.semaphore_wait(barrier, n_tm + 1)

    @pl.when(jnp.logical_not(between))
    def _():
        pl.semaphore_wait(barrier, n_tm)

    def home_copies(b, first=None, last=None):
        view = pl.ds(PAD, height)
        first = home.at[b, :, 1, view, :] if first is None else first
        last = home.at[b, :, depth, view, :] if last is None else last
        down = pltpu.make_async_remote_copy(
            first, home.at[b, :, depth + 1, view, :], home_send.at[b, 0], home_recv.at[b, 0],
            device_id=(t, s - 1), device_id_type=MESH,
        )
        up = pltpu.make_async_remote_copy(
            last, home.at[b, :, 0, view, :], home_send.at[b, 1], home_recv.at[b, 1],
            device_id=(t, s + 1), device_id_type=MESH,
        )
        return down, up

    def start_pair(copies, low, high):
        @pl.when(low)
        def _():
            copies[0].start()

        @pl.when(high)
        def _():
            copies[1].start()

    def wait_pair(copies, low, high):
        @pl.when(low)
        def _():
            copies[0].wait_send()
            copies[1].wait_recv()

        @pl.when(high)
        def _():
            copies[1].wait_send()
            copies[0].wait_recv()

    def home_edges(b):
        start_pair(home_copies(b), lower_x, upper_x)

    def home_wait(b):
        wait_pair(home_copies(b), lower_x, upper_x)

    first_edges = home_copies(0, guess.at[0, :, 0], guess.at[0, :, depth - 1])
    start_pair(first_edges, lower_x, upper_x)

    def moves(which, src, dst):
        return [
            pltpu.make_async_remote_copy(
                src(wrap(t + i)), dst(t), move_send.at[which, i], move_recv.at[which, t],
                device_id=(wrap(t + i), s), device_id_type=MESH,
            )
            for i in range(1, n_tm)
        ]

    def start_moves(which, src, dst):
        pltpu.make_async_copy(src(t), dst(t), move_recv.at[which, t]).start()
        for copy in moves(which, src, dst):
            copy.start()

    def wait_moves(which, dst, index):
        pltpu.make_async_copy(dst(index), dst(index), move_recv.at[which, index]).wait()

    def source_rows(i):
        return lambda j: source.at[i, :, :, block(j), :]

    def u_rows(j):
        return home.at[2, :, pl.ds(1, depth), home_block(j), :]

    def u_slot(j):
        return state.at[0, wrap(j + 1), :, pl.ds(1, depth), pl.ds(PAD, rows), :]

    def f0_slot(j):
        return force0.at[j]

    def f1_slot(j):
        return force1.at[j]

    start_moves(0, source_rows(0), f0_slot)

    def lookup(ids, table):
        value = jnp.zeros(ids.shape, jnp.float32)
        for i in range(table.shape[0]):
            value = jnp.where(ids == i, table[i], value)
        return value

    my_rows = pl.ds(pl.multiple_of(p * rows, 8), rows)

    @pl.loop(0, depth)
    def _(x):
        ids = regions[x]
        home_cond[x] = lookup(ids, conductance)
        home_nu[x] = lookup(ids, reluct)
        c = home_cond[x, my_rows, :]
        n = home_nu[x, my_rows, :]
        cond[x] = c
        nu0[x] = n
        half = c / steps
        inverse = 1.0 / (half + 6.0 * n)
        w_old[x] = half * inverse
        w_sum[x] = n * inverse

    chunk = 32 if height % 32 == 0 else height

    def home_sweep(b, first):
        @pl.loop(0, depth)
        def _(x):
            for r0 in range(0, height, chunk):
                cut = pl.ds(r0, chunk)
                centre, total = neighbour_sum(home.at[b], x, 1, r0, chunk, None)
                c, n = home_cond[pl.ds(x, 1), cut, :], home_nu[pl.ds(x, 1), cut, :]
                if first:
                    k = c[None] * centre + home_force[:, pl.ds(x, 1), cut, :]
                    home_known[:, pl.ds(x, 1), cut, :] = k
                else:
                    k = home_known[:, pl.ds(x, 1), cut, :]
                home[b + 1, :, pl.ds(x + 1, 1), pl.ds(PAD + r0, chunk), :] = fine(centre, total, k, c, n)

    load_guess.wait()
    load_force.wait()
    wait_pair(first_edges, lower_x, upper_x)
    home_sweep(0, True)
    home_edges(1)
    home_wait(1)
    home_sweep(1, False)
    start_moves(1, u_rows, u_slot)
    start_moves(2, source_rows(1), f1_slot)

    def halo_copies(b, k):
        view = pl.ds(PAD, rows)
        tm_low, tm_high = place(p - 1, n_tm), place(p + 1, n_tm)
        x_down = pltpu.make_async_remote_copy(
            state.at[b, k, :, 1, view, :], state.at[b, k, :, depth + 1, view, :],
            halo_send.at[b, k, 0], halo_recv.at[b, k, 0], device_id=(t, s - 1), device_id_type=MESH,
        )
        x_up = pltpu.make_async_remote_copy(
            state.at[b, k, :, depth, view, :], state.at[b, k, :, 0, view, :],
            halo_send.at[b, k, 1], halo_recv.at[b, k, 1], device_id=(t, s + 1), device_id_type=MESH,
        )
        y_down = pltpu.make_async_remote_copy(
            row_out.at[b, k, 0], row_in.at[b, k, 1],
            halo_send.at[b, k, 2], halo_recv.at[b, k, 2], device_id=(tm_low, s), device_id_type=MESH,
        )
        y_up = pltpu.make_async_remote_copy(
            row_out.at[b, k, 1], row_in.at[b, k, 0],
            halo_send.at[b, k, 3], halo_recv.at[b, k, 3], device_id=(tm_high, s), device_id_type=MESH,
        )
        return (x_down, x_up), (y_down, y_up)

    def send_halo(b, k):
        along_x, along_y = halo_copies(b, k)
        start_pair(along_y, lower_y, upper_y)
        start_pair(along_x, lower_x, upper_x)

    def wait_halo(b, k):
        along_x, along_y = halo_copies(b, k)
        wait_pair(along_y, lower_y, upper_y)
        wait_pair(along_x, lower_x, upper_x)

    layers = 2 if depth % 2 == 0 else 1

    def keep_rows(b, k, x, values):
        for c in range(3):
            for i in range(layers):
                row_out[b, k, 0, pl.ds(c * depth + x + i, 1), :] = values[c, i, 0:1, :]
                row_out[b, k, 1, pl.ds(c * depth + x + i, 1), :] = values[c, i, rows - 1:rows, :]

    def sweep(b, b_out, kind, first, shift, keep):
        @pl.loop(0, n_tm)
        def _(k):
            k_in = wrap(k - 1) if shift else k
            wait_halo(b, k_in)
            halo = (row_in.at[b, k_in, 0], row_in.at[b, k_in, 1], depth)

            @pl.loop(0, depth // layers)
            def _(step):
                x = step * layers
                cut = pl.ds(x, layers)
                centre, total = neighbour_sum(state.at[b, k_in], x, layers, 0, rows, halo)
                if kind == "coarse":
                    k_now = w_old[cut][None] * centre if first else known[k, :, cut]
                    value = k_now + w_sum[cut][None] * total
                else:
                    c, n = cond[cut], nu0[cut]
                    forces = force0 if kind == "force0" else force1
                    k_now = c[None] * centre + forces[k, :, cut] if first else known[k, :, cut]
                    value = fine(centre, total, k_now, c, n)
                if first:
                    known[k, :, cut] = k_now
                if keep == "points":
                    points[k, :, cut] = value
                elif keep == "residual":
                    value = value - points[k, :, cut]
                    res[k, :, cut] = value
                elif keep == "correction":
                    value = value + res[k, :, cut]
                elif keep == "final":
                    out0[k, :, cut] = points[k, :, cut] + (value + res[k, :, cut])
                if keep != "final":
                    state[b_out, k, :, pl.ds(x + 1, layers), pl.ds(PAD, rows), :] = value
                    keep_rows(b_out, k, x, value)

            if keep != "final":
                send_halo(b_out, k)
            if keep == "residual":
                send_back(0, k)
            if keep == "final":
                send_back(1, k)

    def back_view(which, index):
        if which == 0:
            return residual.at[0, :, :, block(index), :]
        return home.at[0, :, pl.ds(1, depth), home_block(index), :]

    def back_source(which, k):
        return res.at[k] if which == 0 else out0.at[k]

    def back_copy(which, k):
        return pltpu.make_async_remote_copy(
            back_source(which, k), back_view(which, t), back_send.at[which, k], back_recv.at[which, t],
            device_id=(k, s), device_id_type=MESH,
        )

    def send_back(which, k):
        @pl.when(k == t)
        def _():
            pltpu.make_async_copy(back_source(which, k), back_view(which, t), back_recv.at[which, t]).start()

        @pl.when(k != t)
        def _():
            back_copy(which, k).start()

    def wait_back(which):
        for i in range(n_tm):
            j = wrap(t + i)
            view = back_view(which, j)
            pltpu.make_async_copy(view, view, back_recv.at[which, j]).wait()
            if i:
                back_copy(which, j).wait_send()

    for i in range(n_tm):
        j = wrap(t - i)
        slot = wrap(j + 1)
        wait_moves(1, u_slot, j)

        @pl.loop(0, depth // layers)
        def _(step):
            x = step * layers
            keep_rows(0, slot, x, state[0, slot, :, pl.ds(x + 1, layers), pl.ds(PAD, rows), :])

        send_halo(0, slot)

    for j in range(n_tm):
        wait_moves(0, f0_slot, j)
    sweep(0, 1, "force0", True, False, None)
    sweep(1, 2, "force0", False, False, "points")
    for j in range(n_tm):
        wait_moves(2, f1_slot, j)
    sweep(2, 0, "force1", True, False, None)
    sweep(0, 1, "force1", False, False, None)
    sweep(1, 2, "force0", True, True, None)
    sweep(2, 0, "force0", False, False, "residual")
    b = 0
    for k in range(1, n_tm):
        sweep(b, (b + 1) % 3, "coarse", True, True, None)
        sweep((b + 1) % 3, (b + 2) % 3, "coarse", False, False, "final" if k == n_tm - 1 else "correction")
        b = (b + 2) % 3

    for copy in moves(0, source_rows(0), f0_slot):
        copy.wait_send()
    for copy in moves(1, u_rows, u_slot):
        copy.wait_send()
    for copy in moves(2, source_rows(1), f1_slot):
        copy.wait_send()

    wait_back(1)
    home_edges(0)
    store0 = pltpu.make_async_copy(
        home.at[0, :, pl.ds(1, depth), pl.ds(PAD, height), :], field.at[0], store_sem.at[0]
    )
    store0.start()
    home_wait(0)
    home_sweep(0, True)
    home_edges(1)
    home_wait(1)
    home_sweep(1, False)
    store1 = pltpu.make_async_copy(
        home.at[2, :, pl.ds(1, depth), pl.ds(PAD, height), :], field.at[1], store_sem.at[1]
    )
    store1.start()
    wait_back(0)
    store0.wait()
    store1.wait()


def solution(mesh):
    n_tm, n_space = mesh.shape["tm"], mesh.shape["space"]

    def body(guess, source, regions, conductance, reluct):
        steps, comps, depth, height, lanes = guess.shape
        rows = height // n_tm
        edge_rows = -(-comps * depth // 8) * 8
        f32 = jnp.float32
        whole = (n_tm, comps, depth, rows, lanes)

        def call(*args):
            return kernel(n_tm, n_space, *args)

        return pl.pallas_call(
            call,
            out_shape=(
                jax.ShapeDtypeStruct(guess.shape, f32),
                jax.ShapeDtypeStruct((1,) + guess.shape[1:], f32),
            ),
            in_specs=[
                pl.BlockSpec(memory_space=pl.ANY),
                pl.BlockSpec(memory_space=pl.ANY),
                pl.BlockSpec(memory_space=pltpu.VMEM),
                pl.BlockSpec(memory_space=pltpu.SMEM),
                pl.BlockSpec(memory_space=pltpu.SMEM),
            ],
            out_specs=(pl.BlockSpec(memory_space=pl.ANY), pl.BlockSpec(memory_space=pl.ANY)),
            scratch_shapes=[
                pltpu.VMEM((3, comps, depth + 2, height + 2 * PAD, lanes), f32),
                pltpu.VMEM((comps, depth, height, lanes), f32),
                pltpu.VMEM((comps, depth, height, lanes), f32),
                pltpu.VMEM((depth, height, lanes), f32),
                pltpu.VMEM((depth, height, lanes), f32),
                pltpu.VMEM((3, n_tm, comps, depth + 2, rows + 2 * PAD, lanes), f32),
                pltpu.VMEM(whole, f32),
                pltpu.VMEM(whole, f32),
                pltpu.VMEM(whole, f32),
                pltpu.VMEM(whole, f32),
                pltpu.VMEM(whole, f32),
                pltpu.VMEM(whole, f32),
                pltpu.VMEM((depth, rows, lanes), f32),
                pltpu.VMEM((depth, rows, lanes), f32),
                pltpu.VMEM((depth, rows, lanes), f32),
                pltpu.VMEM((depth, rows, lanes), f32),
                pltpu.VMEM((3, n_tm, 2, edge_rows, lanes), f32),
                pltpu.VMEM((3, n_tm, 2, edge_rows, lanes), f32),
                pltpu.SemaphoreType.DMA((2,)),
                pltpu.SemaphoreType.DMA((2, 2)),
                pltpu.SemaphoreType.DMA((2, 2)),
                pltpu.SemaphoreType.DMA((3, n_tm, 4)),
                pltpu.SemaphoreType.DMA((3, n_tm, 4)),
                pltpu.SemaphoreType.DMA((3, n_tm)),
                pltpu.SemaphoreType.DMA((3, n_tm)),
                pltpu.SemaphoreType.DMA((2, n_tm)),
                pltpu.SemaphoreType.DMA((2, n_tm)),
                pltpu.SemaphoreType.DMA((2,)),
            ],
            compiler_params=pltpu.CompilerParams(
                collective_id=0, has_side_effects=True, vmem_limit_bytes=48 * 1024 * 1024
            ),
        )(guess, source, regions, conductance, reluct)

    in_specs = (
        P("tm", None, "space", None, None),
        P("tm", None, "space", None, None),
        P("space", None, None),
        P(),
        P(),
    )
    out_specs = (P("tm", None, "space", None, None), P("tm", None, "space", None, None))
    return jax.shard_map(body, mesh=mesh, in_specs=in_specs, out_specs=out_specs, check_vma=False)
```

time: 293 us -> 136 us (0.46); the launches traced: 289 us -> 136 us
  waiting for transfers between devices: 140 us -> 0 us
  Pallas kernels: 0 us -> 131 us
  starting transfers between devices: 126 us -> 0 us
  other arithmetic: 19.4 us -> 0 us
    ppermute x42 -> x0, waiting for transfers between devices: 140 us -> none  [the longest x6 117 us: shifted(): return lax.ppermute(block, axis, route)]
    pallas_call x0 -> x1, Pallas kernels: none -> 131 us  [body(): pl.pallas_call(call, out_shape=(jax.ShapeDtypeStruct(guess.shape, f32), j...]
    ppermute x42 -> x0, starting transfers between devices: 126 us -> none  [the longest x18 81 us: extended_2(): before = lax.ppermute(last, axis, up)]
    reduce_sum x11 -> x0, other arithmetic: 6.68 us -> none  [the longest x10 6.34 us: fine_update(): square = jnp.sum(centre * centre, axis=0)]
    add x13 -> x0, other arithmetic: 5.61 us -> none  [the longest x3 4.17 us: body(): correction = coarse_state + residual]
    div x6 -> x0, other arithmetic: 4.56 us -> none  [the longest x4 2.76 us: body(): (cond_coarse * flat + base_nu * neighbour_sum(rim_one(coarse_state))) / (...]
    unnamed x12 -> x8, local copies, waits for them, and re-layouts: 0.25 us -> 4.72 us
  transfers between devices with their start and end apart: 42 -> 0, of which waited for: 36 -> 0; matrix products, arithmetic and copies ran while one was open for 3% -> 0% of each run, Pallas kernels for 0% -> 0%
where the time goes in v1:
time: 136 us
  Pallas kernels  131 us (96%)
  local copies, waits for them, and re-layouts  4.72 us (3%)
    pallas_call x1, Pallas kernels, body(): pl.pallas_call(call, out_shape=(jax.ShapeDtypeStruct(guess.shape, f32), j...  131 us
    unnamed x8, local copies, waits for them, and re-layouts  4.72 us

profile of v1, /device:TPU:7, one launch (start us, length us, event | category | flops | bytes accessed | tf_op | source)
XLA Modules:
  0.0 135.9 jit_solution(15709368422604694499)
XLA Ops:
  0.6 0.0 copy-start
  0.6 1.0 copy-done
  1.6 0.0 copy-start.1
  1.6 0.7 copy-done.1
  2.3 0.0 copy-start.2
  2.3 0.7 copy-done.2
  2.9 130.5 %shard_map.68 = (f32[2,3,12,64,128]{4,3,2,1,0:T(8,128)S(1)}, f32[1,3,12,64,128]{4,3,2,1,0:T(8,128)S(1)}) custom-call(f32[2,3,12,64,128]{4,3,2,1,0:T(8,128)} %args_0_.4, f32[2,3,12,64,128]{4,3,2,1,0:T(8,128)} %args_1_.4, s32[12,64,128]{2,1,0:T(8,128)S(1)} %copy-done, f32[4]{0:T(128)S(1)} %copy-done.1, f32[4]{0:T(128)S(1)} %copy-done.2), custom_call_target="tpu_custom_call" | custom-call | tf_op jit(solution)/shard_map/pallas_call | solution.py:433
  133.5 1.4 %copy.9 = f32[2,3,12,64,128]{4,3,2,1,0:T(8,128)} copy(f32[2,3,12,64,128]{4,3,2,1,0:T(8,128)S(1)} %get-tuple-element.4) | data formatting | bytes 4718592
  134.9 1.0 copy.10
Async XLA Ops:
  0.6 1.0 copy-start
  1.6 0.7 copy-start.1
  2.3 0.7 copy-start.2

commit v2 on v1

--- a/solution.py
+++ b/solution.py
@@ -54,7 +54,9 @@
     s = (centre[0] * centre[0] + centre[1] * centre[1]) + centre[2] * centre[2]
     one = 1.0 + s
     weight = nu0 * (one + 0.5 * s)
-    scale = 1.0 / (cond * one + 6.0 * weight)
+    below = cond * one + 6.0 * weight
+    scale = pl.reciprocal(below, approx=True)
+    scale = scale * (2.0 - below * scale)
     return (known * (one * scale)[None]) + (weight * scale)[None] * total
 
 
@@ -62,8 +64,8 @@
     n_tm, n_space,
     guess, source, regions, conductance, reluct,
     field, residual,
-    home, home_force, home_known, home_cond, home_nu,
-    state, force0, force1, known, points, res, out0,
+    home0, home1, home2, home_force, home_known, home_cond, home_nu,
+    state0, state1, state2, force0, force1, known, points, res, out0,
     cond, nu0, w_old, w_sum,
     row_out, row_in,
     load_sem, home_send, home_recv, halo_send, halo_recv,
@@ -71,6 +73,7 @@
 ):
     steps, _, depth, height, lanes = guess.shape
     rows = height // n_tm
+    home, state = (home0, home1, home2), (state0, state1, state2)
     t, s = lax.axis_index("tm"), lax.axis_index("space")
     p = place(t, n_tm)
     lower_x, upper_x = s > 0, s < n_space - 1
@@ -86,7 +89,7 @@
         return pl.ds(pl.multiple_of(place(index, n_tm) * rows + PAD, 8), rows)
 
     load_guess = pltpu.make_async_copy(
-        guess.at[0], home.at[0, :, pl.ds(1, depth), pl.ds(PAD, height), :], load_sem.at[0]
+        guess.at[0], home[0].at[:, pl.ds(1, depth), pl.ds(PAD, height), :], load_sem.at[0]
     )
     load_force = pltpu.make_async_copy(source.at[1], home_force, load_sem.at[1])
     load_guess.start()
@@ -94,13 +97,13 @@
 
     zero_layer = jnp.zeros((3, height, lanes), jnp.float32)
     for b in range(2):
-        home[b, :, 0, pl.ds(PAD, height), :] = zero_layer
-        home[b, :, depth + 1, pl.ds(PAD, height), :] = zero_layer
+        home[b][:, 0, pl.ds(PAD, height), :] = zero_layer
+        home[b][:, depth + 1, pl.ds(PAD, height), :] = zero_layer
         for r0 in (0, PAD + height):
-            home[b, :, :, pl.ds(r0, PAD), :] = jnp.zeros((3, depth + 2, PAD, lanes), jnp.float32)
+            home[b][:, :, pl.ds(r0, PAD), :] = jnp.zeros((3, depth + 2, PAD, lanes), jnp.float32)
     for b in range(3):
         for layer in (0, depth + 1):
-            state[b, :, :, layer, pl.ds(PAD, rows), :] = jnp.zeros((n_tm, 3, rows, lanes), jnp.float32)
+            state[b][:, :, layer, pl.ds(PAD, rows), :] = jnp.zeros((n_tm, 3, rows, lanes), jnp.float32)
     row_in[...] = jnp.zeros_like(row_in)
 
     barrier = pltpu.get_barrier_semaphore()
@@ -127,14 +130,14 @@
 
     def home_copies(b, first=None, last=None):
         view = pl.ds(PAD, height)
-        first = home.at[b, :, 1, view, :] if first is None else first
-        last = home.at[b, :, depth, view, :] if last is None else last
+        first = home[b].at[:, 1, view, :] if first is None else first
+        last = home[b].at[:, depth, view, :] if last is None else last
         down = pltpu.make_async_remote_copy(
-            first, home.at[b, :, depth + 1, view, :], home_send.at[b, 0], home_recv.at[b, 0],
+            first, home[b].at[:, depth + 1, view, :], home_send.at[b, 0], home_recv.at[b, 0],
             device_id=(t, s - 1), device_id_type=MESH,
         )
         up = pltpu.make_async_remote_copy(
-            last, home.at[b, :, 0, view, :], home_send.at[b, 1], home_recv.at[b, 1],
+            last, home[b].at[:, 0, view, :], home_send.at[b, 1], home_recv.at[b, 1],
             device_id=(t, s + 1), device_id_type=MESH,
         )
         return down, up
@@ -189,10 +192,10 @@
         return lambda j: source.at[i, :, :, block(j), :]
 
     def u_rows(j):
-        return home.at[2, :, pl.ds(1, depth), home_block(j), :]
+        return home[2].at[:, pl.ds(1, depth), home_block(j), :]
 
     def u_slot(j):
-        return state.at[0, wrap(j + 1), :, pl.ds(1, depth), pl.ds(PAD, rows), :]
+        return state[0].at[wrap(j + 1), :, pl.ds(1, depth), pl.ds(PAD, rows), :]
 
     def f0_slot(j):
         return force0.at[j]
@@ -224,21 +227,21 @@
         w_old[x] = half * inverse
         w_sum[x] = n * inverse
 
-    chunk = 32 if height % 32 == 0 else height
+    chunk = height
 
     def home_sweep(b, first):
         @pl.loop(0, depth)
         def _(x):
             for r0 in range(0, height, chunk):
                 cut = pl.ds(r0, chunk)
-                centre, total = neighbour_sum(home.at[b], x, 1, r0, chunk, None)
+                centre, total = neighbour_sum(home[b], x, 1, r0, chunk, None)
                 c, n = home_cond[pl.ds(x, 1), cut, :], home_nu[pl.ds(x, 1), cut, :]
                 if first:
                     k = c[None] * centre + home_force[:, pl.ds(x, 1), cut, :]
                     home_known[:, pl.ds(x, 1), cut, :] = k
                 else:
                     k = home_known[:, pl.ds(x, 1), cut, :]
-                home[b + 1, :, pl.ds(x + 1, 1), pl.ds(PAD + r0, chunk), :] = fine(centre, total, k, c, n)
+                home[b + 1][:, pl.ds(x + 1, 1), pl.ds(PAD + r0, chunk), :] = fine(centre, total, k, c, n)
 
     load_guess.wait()
     load_force.wait()
@@ -254,11 +257,11 @@
         view = pl.ds(PAD, rows)
         tm_low, tm_high = place(p - 1, n_tm), place(p + 1, n_tm)
         x_down = pltpu.make_async_remote_copy(
-            state.at[b, k, :, 1, view, :], state.at[b, k, :, depth + 1, view, :],
+            state[b].at[k, :, 1, view, :], state[b].at[k, :, depth + 1, view, :],
             halo_send.at[b, k, 0], halo_recv.at[b, k, 0], device_id=(t, s - 1), device_id_type=MESH,
         )
         x_up = pltpu.make_async_remote_copy(
-            state.at[b, k, :, depth, view, :], state.at[b, k, :, 0, view, :],
+            state[b].at[k, :, depth, view, :], state[b].at[k, :, 0, view, :],
             halo_send.at[b, k, 1], halo_recv.at[b, k, 1], device_id=(t, s + 1), device_id_type=MESH,
         )
         y_down = pltpu.make_async_remote_copy(
@@ -281,7 +284,7 @@
         wait_pair(along_y, lower_y, upper_y)
         wait_pair(along_x, lower_x, upper_x)
 
-    layers = 2 if depth % 2 == 0 else 1
+    layers = 4 if depth % 4 == 0 else 1
 
     def keep_rows(b, k, x, values):
         for c in range(3):
@@ -300,7 +303,7 @@
             def _(step):
                 x = step * layers
                 cut = pl.ds(x, layers)
-                centre, total = neighbour_sum(state.at[b, k_in], x, layers, 0, rows, halo)
+                centre, total = neighbour_sum(state[b].at[k_in], x, layers, 0, rows, halo)
                 if kind == "coarse":
                     k_now = w_old[cut][None] * centre if first else known[k, :, cut]
                     value = k_now + w_sum[cut][None] * total
@@ -321,7 +324,7 @@
                 elif keep == "final":
                     out0[k, :, cut] = points[k, :, cut] + (value + res[k, :, cut])
                 if keep != "final":
-                    state[b_out, k, :, pl.ds(x + 1, layers), pl.ds(PAD, rows), :] = value
+                    state[b_out][k, :, pl.ds(x + 1, layers), pl.ds(PAD, rows), :] = value
                     keep_rows(b_out, k, x, value)
 
             if keep != "final":
@@ -334,7 +337,7 @@
     def back_view(which, index):
         if which == 0:
             return residual.at[0, :, :, block(index), :]
-        return home.at[0, :, pl.ds(1, depth), home_block(index), :]
+        return home[0].at[:, pl.ds(1, depth), home_block(index), :]
 
     def back_source(which, k):
         return res.at[k] if which == 0 else out0.at[k]
@@ -370,7 +373,7 @@
         @pl.loop(0, depth // layers)
         def _(step):
             x = step * layers
-            keep_rows(0, slot, x, state[0, slot, :, pl.ds(x + 1, layers), pl.ds(PAD, rows), :])
+            keep_rows(0, slot, x, state[0][slot, :, pl.ds(x + 1, layers), pl.ds(PAD, rows), :])
 
         send_halo(0, slot)
 
@@ -400,7 +403,7 @@
     wait_back(1)
     home_edges(0)
     store0 = pltpu.make_async_copy(
-        home.at[0, :, pl.ds(1, depth), pl.ds(PAD, height), :], field.at[0], store_sem.at[0]
+        home[0].at[:, pl.ds(1, depth), pl.ds(PAD, height), :], field.at[0], store_sem.at[0]
     )
     store0.start()
     home_wait(0)
@@ -409,7 +412,7 @@
     home_wait(1)
     home_sweep(1, False)
     store1 = pltpu.make_async_copy(
-        home.at[2, :, pl.ds(1, depth), pl.ds(PAD, height), :], field.at[1], store_sem.at[1]
+        home[2].at[:, pl.ds(1, depth), pl.ds(PAD, height), :], field.at[1], store_sem.at[1]
     )
     store1.start()
     wait_back(0)
@@ -445,12 +448,16 @@
             ],
             out_specs=(pl.BlockSpec(memory_space=pl.ANY), pl.BlockSpec(memory_space=pl.ANY)),
             scratch_shapes=[
-                pltpu.VMEM((3, comps, depth + 2, height + 2 * PAD, lanes), f32),
+                pltpu.VMEM((comps, depth + 2, height + 2 * PAD, lanes), f32),
+                pltpu.VMEM((comps, depth + 2, height + 2 * PAD, lanes), f32),
+                pltpu.VMEM((comps, depth + 2, height + 2 * PAD, lanes), f32),
                 pltpu.VMEM((comps, depth, height, lanes), f32),
                 pltpu.VMEM((comps, depth, height, lanes), f32),
                 pltpu.VMEM((depth, height, lanes), f32),
                 pltpu.VMEM((depth, height, lanes), f32),
-                pltpu.VMEM((3, n_tm, comps, depth + 2, rows + 2 * PAD, lanes), f32),
+                pltpu.VMEM((n_tm, comps, depth + 2, rows + 2 * PAD, lanes), f32),
+                pltpu.VMEM((n_tm, comps, depth + 2, rows + 2 * PAD, lanes), f32),
+                pltpu.VMEM((n_tm, comps, depth + 2, rows + 2 * PAD, lanes), f32),
                 pltpu.VMEM(whole, f32),
                 pltpu.VMEM(whole, f32),
                 pltpu.VMEM(whole, f32),
@@ -475,7 +482,7 @@
                 pltpu.SemaphoreType.DMA((2,)),
             ],
             compiler_params=pltpu.CompilerParams(
-                collective_id=0, has_side_effects=True, vmem_limit_bytes=48 * 1024 * 1024
+                collective_id=0, has_side_effects=True, vmem_limit_bytes=60 * 1024 * 1024
             ),
         )(guess, source, regions, conductance, reluct)
 

time: 136 us -> 132 us (0.971)
  Pallas kernels: 131 us -> 126 us
    pallas_call x1, Pallas kernels: 131 us -> 126 us  [body(): pl.pallas_call(call, out_shape=(jax.ShapeDtypeStruct(guess.shape, f32), j...]
    unnamed x8 -> x4, local copies, waits for them, and re-layouts: 4.72 us -> 4.47 us
where the time goes in v2:
time: 132 us; the launch traced here: 131 us
  Pallas kernels  126 us (95%)
  local copies, waits for them, and re-layouts  4.47 us (3%)
    pallas_call x1, Pallas kernels, body(): pl.pallas_call(call, out_shape=(jax.ShapeDtypeStruct(guess.shape, f32), j...  126 us
    unnamed x4, local copies, waits for them, and re-layouts  4.47 us

profile of v2, /device:TPU:7, one launch (start us, length us, event | category | flops | bytes accessed | tf_op | source)
XLA Modules:
  0.0 131.5 jit_solution(3368850050494687041)
XLA Ops:
  0.6 126.3 %shard_map.68 = (f32[2,3,12,64,128]{4,3,2,1,0:T(8,128)}, f32[1,3,12,64,128]{4,3,2,1,0:T(8,128)}) custom-call(f32[2,3,12,64,128]{4,3,2,1,0:T(8,128)} %args_0_.4, f32[2,3,12,64,128]{4,3,2,1,0:T(8,128)} %args_1_.4, s32[12,64,128]{2,1,0:T(8,128)} %args_2_.4, f32[4]{0:T(128)} %args_3_.4, f32[4]{0:T(128)} %args_4_.4), custom_call_target="tpu_custom_call" | custom-call | tf_op jit(solution)/shard_map/pallas_call | solution.py:436
  127.0 0.0 copy-start
  127.0 3.5 %copy.9 = f32[2,3,12,64,128]{4,3,2,1,0:T(8,128)} copy(f32[2,3,12,64,128]{4,3,2,1,0:T(8,128)} %get-tuple-element.4) | data formatting | bytes 4718592
  130.4 0.0 copy-done
  130.4 1.0 copy.10
Async XLA Ops:
  127.0 3.5 %copy-start = (f32[1,3,12,64,128]{4,3,2,1,0:T(8,128)S(1)}, f32[1,3,12,64,128]{4,3,2,1,0:T(8,128)}, u32[]{:S(2)}) copy-start(f32[1,3,12,64,128]{4,3,2,1,0:T(8,128)} %get-tuple-element.5) | copy-start | bytes 3538948

commit v3 on v2

--- a/solution.py
+++ b/solution.py
@@ -200,8 +200,11 @@
     def f0_slot(j):
         return force0.at[j]
 
-    def f1_slot(j):
-        return force1.at[j]
+    def f1_rows(c):
+        return lambda j: source.at[1, c, :, block(j), :]
+
+    def f1_slot(c):
+        return lambda j: force1.at[j, c]
 
     start_moves(0, source_rows(0), f0_slot)
 
@@ -251,7 +254,6 @@
     home_wait(1)
     home_sweep(1, False)
     start_moves(1, u_rows, u_slot)
-    start_moves(2, source_rows(1), f1_slot)
 
     def halo_copies(b, k):
         view = pl.ds(PAD, rows)
@@ -329,18 +331,22 @@
 
             if keep != "final":
                 send_halo(b_out, k)
-            if keep == "residual":
-                send_back(0, k)
             if keep == "final":
-                send_back(1, k)
+                send_back(len(pieces), k)
+
+    pieces = [(c, slice(h * (depth // 2), depth if h else depth // 2)) for h in range(2) for c in range(3)]
 
     def back_view(which, index):
-        if which == 0:
-            return residual.at[0, :, :, block(index), :]
+        if which < len(pieces):
+            c, cut = pieces[which]
+            return residual.at[0, c, cut, block(index), :]
         return home[0].at[:, pl.ds(1, depth), home_block(index), :]
 
     def back_source(which, k):
-        return res.at[k] if which == 0 else out0.at[k]
+        if which < len(pieces):
+            c, cut = pieces[which]
+            return res.at[k, c, cut]
+        return out0.at[k]
 
     def back_copy(which, k):
         return pltpu.make_async_remote_copy(
@@ -356,6 +362,11 @@
         @pl.when(k != t)
         def _():
             back_copy(which, k).start()
+
+    def send_piece(which):
+        @pl.loop(0, n_tm)
+        def _(k):
+            send_back(which, k)
 
     def wait_back(which):
         for i in range(n_tm):
@@ -377,30 +388,43 @@
 
         send_halo(0, slot)
 
+    start_moves(2, f1_rows(0), f1_slot(0))
     for j in range(n_tm):
         wait_moves(0, f0_slot, j)
     sweep(0, 1, "force0", True, False, None)
+    start_moves(3, f1_rows(1), f1_slot(1))
+    start_moves(4, f1_rows(2), f1_slot(2))
     sweep(1, 2, "force0", False, False, "points")
-    for j in range(n_tm):
-        wait_moves(2, f1_slot, j)
+    for c in range(3):
+        for j in range(n_tm):
+            wait_moves(2 + c, f1_slot(c), j)
     sweep(2, 0, "force1", True, False, None)
     sweep(0, 1, "force1", False, False, None)
     sweep(1, 2, "force0", True, True, None)
     sweep(2, 0, "force0", False, False, "residual")
-    b = 0
+    b, sent = 0, 0
     for k in range(1, n_tm):
         sweep(b, (b + 1) % 3, "coarse", True, True, None)
+        if sent < len(pieces):
+            send_piece(sent)
+            sent += 1
         sweep((b + 1) % 3, (b + 2) % 3, "coarse", False, False, "final" if k == n_tm - 1 else "correction")
+        if sent < len(pieces):
+            send_piece(sent)
+            sent += 1
         b = (b + 2) % 3
+    for which in range(sent, len(pieces)):
+        send_piece(which)
 
     for copy in moves(0, source_rows(0), f0_slot):
         copy.wait_send()
     for copy in moves(1, u_rows, u_slot):
         copy.wait_send()
-    for copy in moves(2, source_rows(1), f1_slot):
-        copy.wait_send()
-
-    wait_back(1)
+    for c in range(3):
+        for copy in moves(2 + c, f1_rows(c), f1_slot(c)):
+            copy.wait_send()
+
+    wait_back(len(pieces))
     home_edges(0)
     store0 = pltpu.make_async_copy(
         home[0].at[:, pl.ds(1, depth), pl.ds(PAD, height), :], field.at[0], store_sem.at[0]
@@ -415,7 +439,8 @@
         home[2].at[:, pl.ds(1, depth), pl.ds(PAD, height), :], field.at[1], store_sem.at[1]
     )
     store1.start()
-    wait_back(0)
+    for which in range(len(pieces)):
+        wait_back(which)
     store0.wait()
     store1.wait()
 
@@ -475,10 +500,10 @@
                 pltpu.SemaphoreType.DMA((2, 2)),
                 pltpu.SemaphoreType.DMA((3, n_tm, 4)),
                 pltpu.SemaphoreType.DMA((3, n_tm, 4)),
-                pltpu.SemaphoreType.DMA((3, n_tm)),
-                pltpu.SemaphoreType.DMA((3, n_tm)),
-                pltpu.SemaphoreType.DMA((2, n_tm)),
-                pltpu.SemaphoreType.DMA((2, n_tm)),
+                pltpu.SemaphoreType.DMA((5, n_tm)),
+                pltpu.SemaphoreType.DMA((5, n_tm)),
+                pltpu.SemaphoreType.DMA((7, n_tm)),
+                pltpu.SemaphoreType.DMA((7, n_tm)),
                 pltpu.SemaphoreType.DMA((2,)),
             ],
             compiler_params=pltpu.CompilerParams(

time: 132 us -> 121 us (0.917)
  Pallas kernels: 126 us -> 116 us
    pallas_call x1, Pallas kernels: 126 us -> 116 us  [body(): pl.pallas_call(call, out_shape=(jax.ShapeDtypeStruct(guess.shape, f32), j...]
where the time goes in v3:
time: 121 us
  Pallas kernels  116 us (96%)
  local copies, waits for them, and re-layouts  4.47 us (4%)
    pallas_call x1, Pallas kernels, body(): pl.pallas_call(call, out_shape=(jax.ShapeDtypeStruct(guess.shape, f32), j...  116 us
    unnamed x4, local copies, waits for them, and re-layouts  4.47 us

profile of v3, /device:TPU:7, one launch (start us, length us, event | category | flops | bytes accessed | tf_op | source)
XLA Modules:
  0.0 120.6 jit_solution(14808435900156913985)
XLA Ops:
  0.6 115.5 %shard_map.68 = (f32[2,3,12,64,128]{4,3,2,1,0:T(8,128)}, f32[1,3,12,64,128]{4,3,2,1,0:T(8,128)}) custom-call(f32[2,3,12,64,128]{4,3,2,1,0:T(8,128)} %args_0_.4, f32[2,3,12,64,128]{4,3,2,1,0:T(8,128)} %args_1_.4, s32[12,64,128]{2,1,0:T(8,128)} %args_2_.4, f32[4]{0:T(128)} %args_3_.4, f32[4]{0:T(128)} %args_4_.4), custom_call_target="tpu_custom_call" | custom-call | tf_op jit(solution)/shard_map/pallas_call | solution.py:461
  116.1 0.0 copy-start
  116.2 3.5 %copy.9 = f32[2,3,12,64,128]{4,3,2,1,0:T(8,128)} copy(f32[2,3,12,64,128]{4,3,2,1,0:T(8,128)} %get-tuple-element.4) | data formatting | bytes 4718592
  119.6 0.0 copy-done
  119.6 1.0 copy.10
Async XLA Ops:
  116.1 3.5 %copy-start = (f32[1,3,12,64,128]{4,3,2,1,0:T(8,128)S(1)}, f32[1,3,12,64,128]{4,3,2,1,0:T(8,128)}, u32[]{:S(2)}) copy-start(f32[1,3,12,64,128]{4,3,2,1,0:T(8,128)} %get-tuple-element.5) | copy-start | bytes 3538948

commit v4 on v3

--- a/solution.py
+++ b/solution.py
@@ -17,31 +17,12 @@
     return index + odd_pair * (1 - 2 * lax.rem(index, 2))
 
 
-def neighbour_sum(state, x, layers, r0, rows, halo):
+def neighbour_sum(state, x, layers, r0, rows):
     middle, lanes = pl.ds(PAD + r0, rows), state.shape[-1]
     centre = state[:, pl.ds(x + 1, layers), middle, :]
     first = state[:, pl.ds(x + 2, layers), middle, :] + state[:, pl.ds(x, layers), middle, :]
     above = state[:, pl.ds(x + 1, layers), pl.ds(PAD + r0 - 1, rows), :]
     below = state[:, pl.ds(x + 1, layers), pl.ds(PAD + r0 + 1, rows), :]
-    if halo is not None:
-        top, bottom, depth = halo
-        row = lax.broadcasted_iota(jnp.int32, (rows, lanes), 0)
-
-        def filled(side, values, at):
-            return jnp.stack([
-                jnp.stack([
-                    jnp.where(
-                        row == at,
-                        jnp.broadcast_to(side[pl.ds(c * depth + x + i, 1), :], (rows, lanes)),
-                        values[c, i],
-                    )
-                    for i in range(layers)
-                ])
-                for c in range(3)
-            ])
-
-        above = filled(top, above, 0)
-        below = filled(bottom, below, rows - 1)
     flat = centre.reshape(-1, lanes)
     lane = lax.broadcasted_iota(jnp.int32, flat.shape, 1)
     left = jnp.where(lane == 0, 0.0, pltpu.roll(flat, 1, 1))
@@ -67,7 +48,6 @@
     home0, home1, home2, home_force, home_known, home_cond, home_nu,
     state0, state1, state2, force0, force1, known, points, res, out0,
     cond, nu0, w_old, w_sum,
-    row_out, row_in,
     load_sem, home_send, home_recv, halo_send, halo_recv,
     move_send, move_recv, back_send, back_recv, store_sem,
 ):
@@ -104,7 +84,8 @@
     for b in range(3):
         for layer in (0, depth + 1):
             state[b][:, :, layer, pl.ds(PAD, rows), :] = jnp.zeros((n_tm, 3, rows, lanes), jnp.float32)
-    row_in[...] = jnp.zeros_like(row_in)
+        for row in (PAD - 1, PAD + rows):
+            state[b][:, :, :, pl.ds(row, 1), :] = jnp.zeros((n_tm, 3, depth + 2, 1, lanes), jnp.float32)
 
     barrier = pltpu.get_barrier_semaphore()
     for i in range(1, n_tm):
@@ -237,7 +218,7 @@
         def _(x):
             for r0 in range(0, height, chunk):
                 cut = pl.ds(r0, chunk)
-                centre, total = neighbour_sum(home[b], x, 1, r0, chunk, None)
+                centre, total = neighbour_sum(home[b], x, 1, r0, chunk)
                 c, n = home_cond[pl.ds(x, 1), cut, :], home_nu[pl.ds(x, 1), cut, :]
                 if first:
                     k = c[None] * centre + home_force[:, pl.ds(x, 1), cut, :]
@@ -266,12 +247,13 @@
             state[b].at[k, :, depth, view, :], state[b].at[k, :, 0, view, :],
             halo_send.at[b, k, 1], halo_recv.at[b, k, 1], device_id=(t, s + 1), device_id_type=MESH,
         )
+        inner = pl.ds(1, depth)
         y_down = pltpu.make_async_remote_copy(
-            row_out.at[b, k, 0], row_in.at[b, k, 1],
+            state[b].at[k, :, inner, pl.ds(PAD, 1), :], state[b].at[k, :, inner, pl.ds(PAD + rows, 1), :],
             halo_send.at[b, k, 2], halo_recv.at[b, k, 2], device_id=(tm_low, s), device_id_type=MESH,
         )
         y_up = pltpu.make_async_remote_copy(
-            row_out.at[b, k, 1], row_in.at[b, k, 0],
+            state[b].at[k, :, inner, pl.ds(PAD + rows - 1, 1), :], state[b].at[k, :, inner, pl.ds(PAD - 1, 1), :],
             halo_send.at[b, k, 3], halo_recv.at[b, k, 3], device_id=(tm_high, s), device_id_type=MESH,
         )
         return (x_down, x_up), (y_down, y_up)
@@ -287,25 +269,18 @@
         wait_pair(along_x, lower_x, upper_x)
 
     layers = 4 if depth % 4 == 0 else 1
-
-    def keep_rows(b, k, x, values):
-        for c in range(3):
-            for i in range(layers):
-                row_out[b, k, 0, pl.ds(c * depth + x + i, 1), :] = values[c, i, 0:1, :]
-                row_out[b, k, 1, pl.ds(c * depth + x + i, 1), :] = values[c, i, rows - 1:rows, :]
 
     def sweep(b, b_out, kind, first, shift, keep):
         @pl.loop(0, n_tm)
         def _(k):
             k_in = wrap(k - 1) if shift else k
             wait_halo(b, k_in)
-            halo = (row_in.at[b, k_in, 0], row_in.at[b, k_in, 1], depth)
 
             @pl.loop(0, depth // layers)
             def _(step):
                 x = step * layers
                 cut = pl.ds(x, layers)
-                centre, total = neighbour_sum(state[b].at[k_in], x, layers, 0, rows, halo)
+                centre, total = neighbour_sum(state[b].at[k_in], x, layers, 0, rows)
                 if kind == "coarse":
                     k_now = w_old[cut][None] * centre if first else known[k, :, cut]
                     value = k_now + w_sum[cut][None] * total
@@ -327,7 +302,6 @@
                     out0[k, :, cut] = points[k, :, cut] + (value + res[k, :, cut])
                 if keep != "final":
                     state[b_out][k, :, pl.ds(x + 1, layers), pl.ds(PAD, rows), :] = value
-                    keep_rows(b_out, k, x, value)
 
             if keep != "final":
                 send_halo(b_out, k)
@@ -380,11 +354,6 @@
         j = wrap(t - i)
         slot = wrap(j + 1)
         wait_moves(1, u_slot, j)
-
-        @pl.loop(0, depth // layers)
-        def _(step):
-            x = step * layers
-            keep_rows(0, slot, x, state[0][slot, :, pl.ds(x + 1, layers), pl.ds(PAD, rows), :])
 
         send_halo(0, slot)
 
@@ -451,7 +420,6 @@
     def body(guess, source, regions, conductance, reluct):
         steps, comps, depth, height, lanes = guess.shape
         rows = height // n_tm
-        edge_rows = -(-comps * depth // 8) * 8
         f32 = jnp.float32
         whole = (n_tm, comps, depth, rows, lanes)
 
@@ -493,8 +461,6 @@
                 pltpu.VMEM((depth, rows, lanes), f32),
                 pltpu.VMEM((depth, rows, lanes), f32),
                 pltpu.VMEM((depth, rows, lanes), f32),
-                pltpu.VMEM((3, n_tm, 2, edge_rows, lanes), f32),
-                pltpu.VMEM((3, n_tm, 2, edge_rows, lanes), f32),
                 pltpu.SemaphoreType.DMA((2,)),
                 pltpu.SemaphoreType.DMA((2, 2)),
                 pltpu.SemaphoreType.DMA((2, 2)),
@@ -507,7 +473,7 @@
                 pltpu.SemaphoreType.DMA((2,)),
             ],
             compiler_params=pltpu.CompilerParams(
-                collective_id=0, has_side_effects=True, vmem_limit_bytes=60 * 1024 * 1024
+                collective_id=0, has_side_effects=True, vmem_limit_bytes=54 * 1024 * 1024
             ),
         )(guess, source, regions, conductance, reluct)
 

time: 121 us -> 120 us (level)
  no operation moved by 1% of the time
where the time goes in v4:
time: 120 us
  Pallas kernels  115 us (96%)
  local copies, waits for them, and re-layouts  4.47 us (4%)
    pallas_call x1, Pallas kernels, body(): pl.pallas_call(call, out_shape=(jax.ShapeDtypeStruct(guess.shape, f32), j...  115 us
    unnamed x4, local copies, waits for them, and re-layouts  4.47 us

profile of v4, /device:TPU:7, one launch (start us, length us, event | category | flops | bytes accessed | tf_op | source)
XLA Modules:
  0.0 120.3 jit_solution(9183013455863136191)
XLA Ops:
  0.6 115.2 %shard_map.68 = (f32[2,3,12,64,128]{4,3,2,1,0:T(8,128)}, f32[1,3,12,64,128]{4,3,2,1,0:T(8,128)}) custom-call(f32[2,3,12,64,128]{4,3,2,1,0:T(8,128)} %args_0_.4, f32[2,3,12,64,128]{4,3,2,1,0:T(8,128)} %args_1_.4, s32[12,64,128]{2,1,0:T(8,128)} %args_2_.4, f32[4]{0:T(128)} %args_3_.4, f32[4]{0:T(128)} %args_4_.4), custom_call_target="tpu_custom_call" | custom-call | tf_op jit(solution)/shard_map/pallas_call | solution.py:429
  115.9 0.0 copy-start
  115.9 3.5 %copy.9 = f32[2,3,12,64,128]{4,3,2,1,0:T(8,128)} copy(f32[2,3,12,64,128]{4,3,2,1,0:T(8,128)} %get-tuple-element.4) | data formatting | bytes 4718592
  119.3 0.0 copy-done
  119.3 1.0 copy.10
Async XLA Ops:
  115.9 3.5 %copy-start = (f32[1,3,12,64,128]{4,3,2,1,0:T(8,128)S(1)}, f32[1,3,12,64,128]{4,3,2,1,0:T(8,128)}, u32[]{:S(2)}) copy-start(f32[1,3,12,64,128]{4,3,2,1,0:T(8,128)} %get-tuple-element.5) | copy-start | bytes 3538948

commit v5 on v4

--- a/solution.py
+++ b/solution.py
@@ -7,6 +7,7 @@
 
 PICARD = 2
 MESH = pl.DeviceIdType.MESH
+BESIDE_COARSE = 2
 PAD = 8
 
 
@@ -146,9 +147,6 @@
     def home_edges(b):
         start_pair(home_copies(b), lower_x, upper_x)
 
-    def home_wait(b):
-        wait_pair(home_copies(b), lower_x, upper_x)
-
     first_edges = home_copies(0, guess.at[0, :, 0], guess.at[0, :, depth - 1])
     start_pair(first_edges, lower_x, upper_x)
 
@@ -211,29 +209,32 @@
         w_old[x] = half * inverse
         w_sum[x] = n * inverse
 
-    chunk = height
-
-    def home_sweep(b, first):
-        @pl.loop(0, depth)
+    def home_sweep(b, first, copies):
+        def layer(x):
+            centre, total = neighbour_sum(home[b], x, 1, 0, height)
+            c, n = home_cond[pl.ds(x, 1)], home_nu[pl.ds(x, 1)]
+            if first:
+                k = c[None] * centre + home_force[:, pl.ds(x, 1)]
+                home_known[:, pl.ds(x, 1)] = k
+            else:
+                k = home_known[:, pl.ds(x, 1)]
+            home[b + 1][:, pl.ds(x + 1, 1), pl.ds(PAD, height), :] = fine(centre, total, k, c, n)
+
+        @pl.loop(1, depth - 1)
         def _(x):
-            for r0 in range(0, height, chunk):
-                cut = pl.ds(r0, chunk)
-                centre, total = neighbour_sum(home[b], x, 1, r0, chunk)
-                c, n = home_cond[pl.ds(x, 1), cut, :], home_nu[pl.ds(x, 1), cut, :]
-                if first:
-                    k = c[None] * centre + home_force[:, pl.ds(x, 1), cut, :]
-                    home_known[:, pl.ds(x, 1), cut, :] = k
-                else:
-                    k = home_known[:, pl.ds(x, 1), cut, :]
-                home[b + 1][:, pl.ds(x + 1, 1), pl.ds(PAD + r0, chunk), :] = fine(centre, total, k, c, n)
+            layer(x)
+
+        wait_pair(copies, lower_x, upper_x)
+
+        @pl.loop(0, 2)
+        def _(i):
+            layer(i * (depth - 1))
 
     load_guess.wait()
     load_force.wait()
-    wait_pair(first_edges, lower_x, upper_x)
-    home_sweep(0, True)
+    home_sweep(0, True, first_edges)
     home_edges(1)
-    home_wait(1)
-    home_sweep(1, False)
+    home_sweep(1, False, home_copies(1))
     start_moves(1, u_rows, u_slot)
 
     def halo_copies(b, k):
@@ -270,10 +271,11 @@
 
     layers = 4 if depth % 4 == 0 else 1
 
-    def sweep(b, b_out, kind, first, shift, keep):
+    def sweep(b, b_out, kind, first, offset, shift, keep):
         @pl.loop(0, n_tm)
-        def _(k):
-            k_in = wrap(k - 1) if shift else k
+        def _(turn):
+            k_in = lax.rem(turn + offset, n_tm)
+            k = lax.rem(k_in + 1, n_tm) if shift else k_in
             wait_halo(b, k_in)
 
             @pl.loop(0, depth // layers)
@@ -350,39 +352,33 @@
             if i:
                 back_copy(which, j).wait_send()
 
-    for i in range(n_tm):
-        j = wrap(t - i)
-        slot = wrap(j + 1)
-        wait_moves(1, u_slot, j)
-
+    for slot in range(n_tm):
+        wait_moves(1, u_slot, (slot - 1) % n_tm)
         send_halo(0, slot)
 
     start_moves(2, f1_rows(0), f1_slot(0))
     for j in range(n_tm):
         wait_moves(0, f0_slot, j)
-    sweep(0, 1, "force0", True, False, None)
+    sweep(0, 1, "force0", True, 0, False, None)
     start_moves(3, f1_rows(1), f1_slot(1))
     start_moves(4, f1_rows(2), f1_slot(2))
-    sweep(1, 2, "force0", False, False, "points")
+    sweep(1, 2, "force0", False, 0, False, "points")
     for c in range(3):
         for j in range(n_tm):
             wait_moves(2 + c, f1_slot(c), j)
-    sweep(2, 0, "force1", True, False, None)
-    sweep(0, 1, "force1", False, False, None)
-    sweep(1, 2, "force0", True, True, None)
-    sweep(2, 0, "force0", False, False, "residual")
-    b, sent = 0, 0
+    sweep(2, 0, "force1", True, 0, False, None)
+    sweep(0, 1, "force1", False, 0, False, None)
+    sweep(1, 2, "force0", True, 0, True, None)
+    sweep(2, 0, "force0", False, 1, False, "residual")
+    b = 0
     for k in range(1, n_tm):
-        sweep(b, (b + 1) % 3, "coarse", True, True, None)
-        if sent < len(pieces):
-            send_piece(sent)
-            sent += 1
-        sweep((b + 1) % 3, (b + 2) % 3, "coarse", False, False, "final" if k == n_tm - 1 else "correction")
-        if sent < len(pieces):
-            send_piece(sent)
-            sent += 1
+        sweep(b, (b + 1) % 3, "coarse", True, k, True, None)
+        if k <= BESIDE_COARSE:
+            send_piece(k - 1)
+        last = k == n_tm - 1
+        sweep((b + 1) % 3, (b + 2) % 3, "coarse", False, k + 1, False, "final" if last else "correction")
         b = (b + 2) % 3
-    for which in range(sent, len(pieces)):
+    for which in range(min(BESIDE_COARSE, n_tm - 1), len(pieces)):
         send_piece(which)
 
     for copy in moves(0, source_rows(0), f0_slot):
@@ -399,11 +395,9 @@
         home[0].at[:, pl.ds(1, depth), pl.ds(PAD, height), :], field.at[0], store_sem.at[0]
     )
     store0.start()
-    home_wait(0)
-    home_sweep(0, True)
+    home_sweep(0, True, home_copies(0))
     home_edges(1)
-    home_wait(1)
-    home_sweep(1, False)
+    home_sweep(1, False, home_copies(1))
     store1 = pltpu.make_async_copy(
         home[2].at[:, pl.ds(1, depth), pl.ds(PAD, height), :], field.at[1], store_sem.at[1]
     )

time: 120 us -> 114 us (0.950); the launches traced: 120 us -> 113 us
  Pallas kernels: 115 us -> 108 us
    pallas_call x1, Pallas kernels: 115 us -> 108 us  [body(): pl.pallas_call(call, out_shape=(jax.ShapeDtypeStruct(guess.shape, f32), j...]
where the time goes in v5:
time: 114 us; the launch traced here: 113 us
  Pallas kernels  108 us (95%)
  local copies, waits for them, and re-layouts  4.47 us (4%)
    pallas_call x1, Pallas kernels, body(): pl.pallas_call(call, out_shape=(jax.ShapeDtypeStruct(guess.shape, f32), j...  108 us
    unnamed x4, local copies, waits for them, and re-layouts  4.47 us

profile of v5, /device:TPU:7, one launch (start us, length us, event | category | flops | bytes accessed | tf_op | source)
XLA Modules:
  0.0 112.8 jit_solution(10286037852728636002)
XLA Ops:
  0.6 107.7 %shard_map.68 = (f32[2,3,12,64,128]{4,3,2,1,0:T(8,128)}, f32[1,3,12,64,128]{4,3,2,1,0:T(8,128)}) custom-call(f32[2,3,12,64,128]{4,3,2,1,0:T(8,128)} %args_0_.4, f32[2,3,12,64,128]{4,3,2,1,0:T(8,128)} %args_1_.4, s32[12,64,128]{2,1,0:T(8,128)} %args_2_.4, f32[4]{0:T(128)} %args_3_.4, f32[4]{0:T(128)} %args_4_.4), custom_call_target="tpu_custom_call" | custom-call | tf_op jit(solution)/shard_map/pallas_call | solution.py:423
  108.3 0.0 copy-start
  108.3 3.5 %copy.9 = f32[2,3,12,64,128]{4,3,2,1,0:T(8,128)} copy(f32[2,3,12,64,128]{4,3,2,1,0:T(8,128)} %get-tuple-element.4) | data formatting | bytes 4718592
  111.8 0.0 copy-done
  111.8 1.0 copy.10
Async XLA Ops:
  108.3 3.5 %copy-start = (f32[1,3,12,64,128]{4,3,2,1,0:T(8,128)S(1)}, f32[1,3,12,64,128]{4,3,2,1,0:T(8,128)}, u32[]{:S(2)}) copy-start(f32[1,3,12,64,128]{4,3,2,1,0:T(8,128)} %get-tuple-element.5) | copy-start | bytes 3538948

commit v6 on v5

--- a/solution.py
+++ b/solution.py
@@ -76,18 +76,6 @@
     load_guess.start()
     load_force.start()
 
-    zero_layer = jnp.zeros((3, height, lanes), jnp.float32)
-    for b in range(2):
-        home[b][:, 0, pl.ds(PAD, height), :] = zero_layer
-        home[b][:, depth + 1, pl.ds(PAD, height), :] = zero_layer
-        for r0 in (0, PAD + height):
-            home[b][:, :, pl.ds(r0, PAD), :] = jnp.zeros((3, depth + 2, PAD, lanes), jnp.float32)
-    for b in range(3):
-        for layer in (0, depth + 1):
-            state[b][:, :, layer, pl.ds(PAD, rows), :] = jnp.zeros((n_tm, 3, rows, lanes), jnp.float32)
-        for row in (PAD - 1, PAD + rows):
-            state[b][:, :, :, pl.ds(row, 1), :] = jnp.zeros((n_tm, 3, depth + 2, 1, lanes), jnp.float32)
-
     barrier = pltpu.get_barrier_semaphore()
     for i in range(1, n_tm):
         pl.semaphore_signal(barrier, inc=1, device_id=(wrap(t + i), s), device_id_type=MESH)
@@ -133,16 +121,23 @@
         def _():
             copies[1].start()
 
-    def wait_pair(copies, low, high):
+    def wait_arrived(copies, low, high):
         @pl.when(low)
         def _():
+            copies[1].wait_recv()
+
+        @pl.when(high)
+        def _():
+            copies[0].wait_recv()
+
+    def wait_sent(copies, low, high):
+        @pl.when(low)
+        def _():
             copies[0].wait_send()
-            copies[1].wait_recv()
 
         @pl.when(high)
         def _():
             copies[1].wait_send()
-            copies[0].wait_recv()
 
     def home_edges(b):
         start_pair(home_copies(b), lower_x, upper_x)
@@ -186,6 +181,34 @@
         return lambda j: force1.at[j, c]
 
     start_moves(0, source_rows(0), f0_slot)
+
+    @pl.when(jnp.logical_not(lower_x))
+    def _():
+        for b in range(2):
+            home[b][:, 0, pl.ds(PAD, height), :] = jnp.zeros((3, height, lanes), jnp.float32)
+        for b in range(3):
+            state[b][:, :, 0, pl.ds(PAD, rows), :] = jnp.zeros((n_tm, 3, rows, lanes), jnp.float32)
+
+    @pl.when(jnp.logical_not(upper_x))
+    def _():
+        for b in range(2):
+            home[b][:, depth + 1, pl.ds(PAD, height), :] = jnp.zeros((3, height, lanes), jnp.float32)
+        for b in range(3):
+            state[b][:, :, depth + 1, pl.ds(PAD, rows), :] = jnp.zeros((n_tm, 3, rows, lanes), jnp.float32)
+
+    @pl.when(jnp.logical_not(lower_y))
+    def _():
+        for b in range(3):
+            state[b][:, :, :, pl.ds(PAD - 1, 1), :] = jnp.zeros((n_tm, 3, depth + 2, 1, lanes), jnp.float32)
+
+    @pl.when(jnp.logical_not(upper_y))
+    def _():
+        for b in range(3):
+            state[b][:, :, :, pl.ds(PAD + rows, 1), :] = jnp.zeros((n_tm, 3, depth + 2, 1, lanes), jnp.float32)
+
+    for b in range(2):
+        for row in (PAD - 1, PAD + height):
+            home[b][:, :, pl.ds(row, 1), :] = jnp.zeros((3, depth + 2, 1, lanes), jnp.float32)
 
     def lookup(ids, table):
         value = jnp.zeros(ids.shape, jnp.float32)
@@ -224,11 +247,13 @@
         def _(x):
             layer(x)
 
-        wait_pair(copies, lower_x, upper_x)
+        wait_arrived(copies, lower_x, upper_x)
 
         @pl.loop(0, 2)
         def _(i):
             layer(i * (depth - 1))
+
+        wait_sent(copies, lower_x, upper_x)
 
     load_guess.wait()
     load_force.wait()
@@ -264,22 +289,17 @@
         start_pair(along_y, lower_y, upper_y)
         start_pair(along_x, lower_x, upper_x)
 
-    def wait_halo(b, k):
-        along_x, along_y = halo_copies(b, k)
-        wait_pair(along_y, lower_y, upper_y)
-        wait_pair(along_x, lower_x, upper_x)
-
-    layers = 4 if depth % 4 == 0 else 1
+    layers = 4 if depth % 4 == 0 and depth > 4 else 1
 
     def sweep(b, b_out, kind, first, offset, shift, keep):
         @pl.loop(0, n_tm)
         def _(turn):
             k_in = lax.rem(turn + offset, n_tm)
             k = lax.rem(k_in + 1, n_tm) if shift else k_in
-            wait_halo(b, k_in)
-
-            @pl.loop(0, depth // layers)
-            def _(step):
+            along_x, along_y = halo_copies(b, k_in)
+            wait_arrived(along_y, lower_y, upper_y)
+
+            def work(step):
                 x = step * layers
                 cut = pl.ds(x, layers)
                 centre, total = neighbour_sum(state[b].at[k_in], x, layers, 0, rows)
@@ -305,8 +325,20 @@
                 if keep != "final":
                     state[b_out][k, :, pl.ds(x + 1, layers), pl.ds(PAD, rows), :] = value
 
+            @pl.loop(1, depth // layers - 1)
+            def _(step):
+                work(step)
+
+            wait_arrived(along_x, lower_x, upper_x)
+
+            @pl.loop(0, 2)
+            def _(i):
+                work(i * (depth // layers - 1))
+
             if keep != "final":
                 send_halo(b_out, k)
+            wait_sent(along_y, lower_y, upper_y)
+            wait_sent(along_x, lower_x, upper_x)
             if keep == "final":
                 send_back(len(pieces), k)
 

time: 114 us -> 113 us (level)
  Pallas kernels: 108 us -> 106 us
    pallas_call x1, Pallas kernels: 108 us -> 106 us  [body(): pl.pallas_call(call, out_shape=(jax.ShapeDtypeStruct(guess.shape, f32), j...]
where the time goes in v6:
time: 113 us; the launch traced here: 111 us
  Pallas kernels  106 us (94%)
  local copies, waits for them, and re-layouts  4.47 us (4%)
    pallas_call x1, Pallas kernels, body(): pl.pallas_call(call, out_shape=(jax.ShapeDtypeStruct(guess.shape, f32), j...  106 us
    unnamed x4, local copies, waits for them, and re-layouts  4.47 us

profile of v6, /device:TPU:7, one launch (start us, length us, event | category | flops | bytes accessed | tf_op | source)
XLA Modules:
  0.0 111.4 jit_solution(4020151609329544259)
XLA Ops:
  0.6 106.2 %shard_map.68 = (f32[2,3,12,64,128]{4,3,2,1,0:T(8,128)}, f32[1,3,12,64,128]{4,3,2,1,0:T(8,128)}) custom-call(f32[2,3,12,64,128]{4,3,2,1,0:T(8,128)} %args_0_.4, f32[2,3,12,64,128]{4,3,2,1,0:T(8,128)} %args_1_.4, s32[12,64,128]{2,1,0:T(8,128)} %args_2_.4, f32[4]{0:T(128)} %args_3_.4, f32[4]{0:T(128)} %args_4_.4), custom_call_target="tpu_custom_call" | custom-call | tf_op jit(solution)/shard_map/pallas_call | solution.py:455
  106.9 0.0 copy-start
  106.9 3.5 %copy.9 = f32[2,3,12,64,128]{4,3,2,1,0:T(8,128)} copy(f32[2,3,12,64,128]{4,3,2,1,0:T(8,128)} %get-tuple-element.4) | data formatting | bytes 4718592
  110.3 0.0 copy-done
  110.3 1.0 copy.10
Async XLA Ops:
  106.9 3.5 %copy-start = (f32[1,3,12,64,128]{4,3,2,1,0:T(8,128)S(1)}, f32[1,3,12,64,128]{4,3,2,1,0:T(8,128)}, u32[]{:S(2)}) copy-start(f32[1,3,12,64,128]{4,3,2,1,0:T(8,128)} %get-tuple-element.5) | copy-start | bytes 3538948

commit v7 on v6

--- a/solution.py
+++ b/solution.py
@@ -262,24 +262,27 @@
     home_sweep(1, False, home_copies(1))
     start_moves(1, u_rows, u_slot)
 
+    group = 2 if n_tm % 2 == 0 else 1
+
     def halo_copies(b, k):
+        g = pl.ds(k * group, group)
         view = pl.ds(PAD, rows)
         tm_low, tm_high = place(p - 1, n_tm), place(p + 1, n_tm)
         x_down = pltpu.make_async_remote_copy(
-            state[b].at[k, :, 1, view, :], state[b].at[k, :, depth + 1, view, :],
+            state[b].at[g, :, 1, view, :], state[b].at[g, :, depth + 1, view, :],
             halo_send.at[b, k, 0], halo_recv.at[b, k, 0], device_id=(t, s - 1), device_id_type=MESH,
         )
         x_up = pltpu.make_async_remote_copy(
-            state[b].at[k, :, depth, view, :], state[b].at[k, :, 0, view, :],
+            state[b].at[g, :, depth, view, :], state[b].at[g, :, 0, view, :],
             halo_send.at[b, k, 1], halo_recv.at[b, k, 1], device_id=(t, s + 1), device_id_type=MESH,
         )
         inner = pl.ds(1, depth)
         y_down = pltpu.make_async_remote_copy(
-            state[b].at[k, :, inner, pl.ds(PAD, 1), :], state[b].at[k, :, inner, pl.ds(PAD + rows, 1), :],
+            state[b].at[g, :, inner, pl.ds(PAD, 1), :], state[b].at[g, :, inner, pl.ds(PAD + rows, 1), :],
             halo_send.at[b, k, 2], halo_recv.at[b, k, 2], device_id=(tm_low, s), device_id_type=MESH,
         )
         y_up = pltpu.make_async_remote_copy(
-            state[b].at[k, :, inner, pl.ds(PAD + rows - 1, 1), :], state[b].at[k, :, inner, pl.ds(PAD - 1, 1), :],
+            state[b].at[g, :, inner, pl.ds(PAD + rows - 1, 1), :], state[b].at[g, :, inner, pl.ds(PAD - 1, 1), :],
             halo_send.at[b, k, 3], halo_recv.at[b, k, 3], device_id=(tm_high, s), device_id_type=MESH,
         )
         return (x_down, x_up), (y_down, y_up)
@@ -291,18 +294,16 @@
 
     layers = 4 if depth % 4 == 0 and depth > 4 else 1
 
-    def sweep(b, b_out, kind, first, offset, shift, keep):
-        @pl.loop(0, n_tm)
-        def _(turn):
-            k_in = lax.rem(turn + offset, n_tm)
-            k = lax.rem(k_in + 1, n_tm) if shift else k_in
-            along_x, along_y = halo_copies(b, k_in)
-            wait_arrived(along_y, lower_y, upper_y)
-
-            def work(step):
+    def sweep(b, b_out, kind, first, offset, keep):
+        @pl.loop(0, n_tm // group)
+        def _(g):
+            along_x, along_y = halo_copies(b, g)
+
+            def work(j, step):
+                k = lax.rem(j + offset, n_tm)
                 x = step * layers
                 cut = pl.ds(x, layers)
-                centre, total = neighbour_sum(state[b].at[k_in], x, layers, 0, rows)
+                centre, total = neighbour_sum(state[b].at[j], x, layers, 0, rows)
                 if kind == "coarse":
                     k_now = w_old[cut][None] * centre if first else known[k, :, cut]
                     value = k_now + w_sum[cut][None] * total
@@ -323,24 +324,31 @@
                 elif keep == "final":
                     out0[k, :, cut] = points[k, :, cut] + (value + res[k, :, cut])
                 if keep != "final":
-                    state[b_out][k, :, pl.ds(x + 1, layers), pl.ds(PAD, rows), :] = value
-
-            @pl.loop(1, depth // layers - 1)
-            def _(step):
-                work(step)
+                    state[b_out][j, :, pl.ds(x + 1, layers), pl.ds(PAD, rows), :] = value
+
+            wait_arrived(along_y, lower_y, upper_y)
+
+            @pl.loop(0, group)
+            def _(i):
+                @pl.loop(1, depth // layers - 1)
+                def _(step):
+                    work(g * group + i, step)
 
             wait_arrived(along_x, lower_x, upper_x)
 
-            @pl.loop(0, 2)
+            @pl.loop(0, group)
             def _(i):
-                work(i * (depth // layers - 1))
+                @pl.loop(0, 2)
+                def _(end):
+                    work(g * group + i, end * (depth // layers - 1))
+
+                if keep == "final":
+                    send_back(len(pieces), lax.rem(g * group + i + offset, n_tm))
 
             if keep != "final":
-                send_halo(b_out, k)
+                send_halo(b_out, g)
             wait_sent(along_y, lower_y, upper_y)
             wait_sent(along_x, lower_x, upper_x)
-            if keep == "final":
-                send_back(len(pieces), k)
 
     pieces = [(c, slice(h * (depth // 2), depth if h else depth // 2)) for h in range(2) for c in range(3)]
 
@@ -384,31 +392,32 @@
             if i:
                 back_copy(which, j).wait_send()
 
-    for slot in range(n_tm):
-        wait_moves(1, u_slot, (slot - 1) % n_tm)
-        send_halo(0, slot)
+    for g in range(n_tm // group):
+        for slot in range(g * group, (g + 1) * group):
+            wait_moves(1, u_slot, (slot - 1) % n_tm)
+        send_halo(0, g)
 
     start_moves(2, f1_rows(0), f1_slot(0))
     for j in range(n_tm):
         wait_moves(0, f0_slot, j)
-    sweep(0, 1, "force0", True, 0, False, None)
+    sweep(0, 1, "force0", True, 0, None)
     start_moves(3, f1_rows(1), f1_slot(1))
     start_moves(4, f1_rows(2), f1_slot(2))
-    sweep(1, 2, "force0", False, 0, False, "points")
+    sweep(1, 2, "force0", False, 0, "points")
     for c in range(3):
         for j in range(n_tm):
             wait_moves(2 + c, f1_slot(c), j)
-    sweep(2, 0, "force1", True, 0, False, None)
-    sweep(0, 1, "force1", False, 0, False, None)
-    sweep(1, 2, "force0", True, 0, True, None)
-    sweep(2, 0, "force0", False, 1, False, "residual")
+    sweep(2, 0, "force1", True, 0, None)
+    sweep(0, 1, "force1", False, 0, None)
+    sweep(1, 2, "force0", True, 1, None)
+    sweep(2, 0, "force0", False, 1, "residual")
     b = 0
     for k in range(1, n_tm):
-        sweep(b, (b + 1) % 3, "coarse", True, k, True, None)
+        sweep(b, (b + 1) % 3, "coarse", True, k + 1, None)
         if k <= BESIDE_COARSE:
             send_piece(k - 1)
         last = k == n_tm - 1
-        sweep((b + 1) % 3, (b + 2) % 3, "coarse", False, k + 1, False, "final" if last else "correction")
+        sweep((b + 1) % 3, (b + 2) % 3, "coarse", False, k + 1, "final" if last else "correction")
         b = (b + 2) % 3
     for which in range(min(BESIDE_COARSE, n_tm - 1), len(pieces)):
         send_piece(which)

time: 113 us -> 118 us (1.044)
  Pallas kernels: 106 us -> 111 us
    pallas_call x1, Pallas kernels: 106 us -> 111 us  [body(): pl.pallas_call(call, out_shape=(jax.ShapeDtypeStruct(guess.shape, f32), j...]
where the time goes in v7:
time: 118 us; the launch traced here: 116 us
  Pallas kernels  111 us (94%)
  local copies, waits for them, and re-layouts  4.47 us (4%)
    pallas_call x1, Pallas kernels, body(): pl.pallas_call(call, out_shape=(jax.ShapeDtypeStruct(guess.shape, f32), j...  111 us
    unnamed x4, local copies, waits for them, and re-layouts  4.47 us

profile of v7, /device:TPU:7, one launch (start us, length us, event | category | flops | bytes accessed | tf_op | source)
XLA Modules:
  0.0 115.8 jit_solution(7042113361353932793)
XLA Ops:
  0.6 110.7 %shard_map.68 = (f32[2,3,12,64,128]{4,3,2,1,0:T(8,128)}, f32[1,3,12,64,128]{4,3,2,1,0:T(8,128)}) custom-call(f32[2,3,12,64,128]{4,3,2,1,0:T(8,128)} %args_0_.4, f32[2,3,12,64,128]{4,3,2,1,0:T(8,128)} %args_1_.4, s32[12,64,128]{2,1,0:T(8,128)} %args_2_.4, f32[4]{0:T(128)} %args_3_.4, f32[4]{0:T(128)} %args_4_.4), custom_call_target="tpu_custom_call" | custom-call | tf_op jit(solution)/shard_map/pallas_call | solution.py:464
  111.3 0.0 copy-start
  111.3 3.5 %copy.9 = f32[2,3,12,64,128]{4,3,2,1,0:T(8,128)} copy(f32[2,3,12,64,128]{4,3,2,1,0:T(8,128)} %get-tuple-element.4) | data formatting | bytes 4718592
  114.8 0.0 copy-done
  114.8 1.0 copy.10
Async XLA Ops:
  111.3 3.5 %copy-start = (f32[1,3,12,64,128]{4,3,2,1,0:T(8,128)S(1)}, f32[1,3,12,64,128]{4,3,2,1,0:T(8,128)}, u32[]{:S(2)}) copy-start(f32[1,3,12,64,128]{4,3,2,1,0:T(8,128)} %get-tuple-element.5) | copy-start | bytes 3538948
